TPU v7x, 32 devices: a whole 2x2x4 slice. The times are simulated.
32 devices in a mesh: section: 2 (over core), dp: 4 (over z), ctx: 4 (over y, x).
Axes of the slice: x: 2, y: 2, z: 4, core: 2. Of those that a mesh axis runs over, the one named last changes fastest.
Arguments:
- tokens: bfloat16 [2, 4, 1024, 1536], P(None, 'dp', 'ctx'), may hold values from -6 to 6
- cotangent: bfloat16 [2, 4, 1024, 1536], P(None, 'dp', 'ctx'), may hold values from -6 to 6
- doc_lengths: int32 [2, 4, 4], P(None, 'dp'), may hold values from 1 to 896, 1024 in all within a row
- norm_gain: float32 [2, 1536], P('section'), may hold values from 0.5 to 1.5
- w_in: bfloat16 [2, 1536, 6448], P('section', ('dp', 'ctx')), may hold values from -0.15625 to 0.15625
- conv_weight: float32 [2, 4, 3328], P('section'), may hold values from -3 to 3
- conv_bias: float32 [2, 3328], P('section'), may hold values from -0.5 to 0.5
- dt_bias: float32 [2, 48], P('section'), may hold values from -6 to -1
- a_log: float32 [2, 48], P('section'), may hold values from -4 to 1.5
- d_skip: float32 [2, 48], P('section'), may hold values from 0.5 to 1.5
- inner_gain: float32 [2, 3072], P('section'), may hold values from 0.5 to 1.5
- w_out: bfloat16 [2, 3072, 1536], P('section', ('dp', 'ctx')), may hold values from -0.109375 to 0.109375
Outputs:
- hidden_states: bfloat16 [2, 2, 4, 1024, 1536], P('section', None, 'dp', 'ctx')
- input_grads: bfloat16 [2, 2, 4, 1024, 1536], P('section', None, 'dp', 'ctx')
- grad_norm_gain: float32 [2, 1536], P('section')
- grad_w_in: float32 [2, 1536, 6448], P('section', ('dp', 'ctx'))
- grad_conv_weight: float32 [2, 4, 3328], P('section')
- grad_conv_bias: float32 [2, 3328], P('section')
- grad_dt_bias: float32 [2, 48], P('section')
- grad_a_log: float32 [2, 48], P('section')
- grad_d_skip: float32 [2, 48], P('section')
- grad_inner_gain: float32 [2, 3072], P('section')
- grad_w_out: float32 [2, 3072, 1536], P('section', ('dp', 'ctx'))
Inputs may be any that keep to these rules, and one draw needn't show every extreme that they name: `doc_lengths`: the 4 lengths of a row sum to 1024; in every row the longest is exactly 896.
All inputs are finite; a program needn't handle non-finite values.
Results may differ from a plain program's by a relative error of at most 0.013.
Values may be sent and summed in bfloat16 or wider, within the bound.
No kernel may reach another device: no remote copies, remote signals or barrier semaphores. Data moves between devices by JAX's collectives and lax.ppermute only.
A program may use at most 320 MiB of HBM per device.

v0:
```python
import functools

import jax
import jax.numpy as jnp
from jax import lax
from jax.experimental import pallas as pl
from jax.experimental.pallas import tpu as pltpu
from jax.sharding import PartitionSpec as P

HEADS = 48
HEAD = 64
STATE = 128
CONV = 4
INNER = 3072
CONV_DIM = 3328
NORM_EPS = 1e-05

F32 = jnp.float32
BF16 = jnp.bfloat16
HIGH = lax.Precision.HIGHEST
CTX = 4
SEGS = 2
LOCAL = HEADS // CTX
WIDE = LOCAL * HEAD
MIX = WIDE + 2 * STATE
FULL = MIX + 128
HALF = WIDE // 2
LOAD = HALF + STATE + 128
PACK = 24
MIB = 1024 * 1024
MICROS = {
    "project": 3,
    "scan_rows": 8,
    "out_rows": 4,
    "gate_back": 3,
    "scan_back": 16,
    "input_back": 4,
    "grad_gate": 8,
    "grad_conv": 6,
}


def swap_core(x):
    return lax.ppermute(x, "section", [(0, 1), (1, 0)])


def flip(x, bits):
    return lax.ppermute(x, "ctx", [(i, i ^ bits) for i in range(CTX)])


def gather_slots(order, own, extra=0):
    half = (own.shape[0] - extra) // 2
    x, y = flip(own, 1), flip(own, 2)

    def forward():
        order.after((x, y))
        first, second = order.now(y[: extra + half]), order.now(x[extra + half :])
        return [own, x, y, flip(first, 1), flip(second, 2)]

    return forward


def scatter_start(own, to_x, to_y, late_x, late_y):
    return own, flip(to_x, 1), flip(to_y, 2), late_x, late_y


def scatter_slots(order, own, from_x, from_y, late_x, late_y):
    extra = from_x.shape[0] - 2 * late_x.shape[0]
    outs = [shape((late_x.shape[0] + extra, late_x.shape[1]), BF16), late_y]
    late_x, late_y = order(call_with("turn", turn_kernel, [from_x, from_y, late_x, late_y], outs))
    return [own, from_x, from_y, flip(late_x, 1), flip(late_y, 2)]


def from_all(x):
    return [x] + [flip(x, m) for m in range(1, CTX)]


def dot(a, b, dims, precision=None):
    return lax.dot_general(a, b, (dims, ((), ())), precision=precision, preferred_element_type=F32)


AB = ((1,), (0,))
ABT = ((1,), (1,))
ATB = ((0,), (0,))


def far(x):
    return pltpu.with_memory_space_constraint(x, pltpu.HBM)


def call_with(name, kernel, ins, outs):
    return lambda sp: call(name, kernel, sp, ins, outs)


def split_dot(a, b, dims):
    a_high, b_high = a.astype(BF16), b.astype(BF16)
    a_low = (a - a_high.astype(F32)).astype(BF16)
    b_low = (b - b_high.astype(F32)).astype(BF16)
    return dot(a_high, b_high, dims) + dot(a_low, b_high, dims) + dot(a_high, b_low, dims)


def whole(x):
    zeros = (0,) * len(x.shape)
    return pl.BlockSpec(tuple(x.shape), lambda i, sp: zeros)


def shape(dims, dtype):
    return jax.ShapeDtypeStruct(dims, dtype)


def call(name, kernel, sp, ins, outs, vmem=20, grid=1, scratch=()):
    ins = [x if isinstance(x, tuple) else (x, whole(x)) for x in ins]
    outs = [x if isinstance(x, tuple) else (x, whole(x)) for x in outs]
    return pl.pallas_call(
        kernel,
        grid_spec=pltpu.PrefetchScalarGridSpec(
            num_scalar_prefetch=1,
            grid=(grid,),
            in_specs=[spec for _, spec in ins],
            out_specs=[spec for _, spec in outs],
            scratch_shapes=list(scratch),
        ),
        out_shape=[x for x, _ in outs],
        compiler_params=pltpu.CompilerParams(
            dimension_semantics=("arbitrary",), vmem_limit_bytes=vmem * MIB
        ),
        cost_estimate=pl.CostEstimate(
            flops=int(MICROS.get(name, 1) * 1e9), bytes_accessed=1, transcendentals=0
        ),
        name=name,
    )(sp, *[x for x, _ in ins])


def natural_spec(x, seg, slot):
    def at(i, sp):
        inside = slot ^ sp[0]
        return (2 * seg + (inside >> 1)) ^ sp[0], inside & 1, 0, 0

    return pl.BlockSpec((1, 1) + x.shape[2:], at)


def natural_slots(x, seg):
    x = far(x)
    return [(x, natural_spec(x, seg, m)) for m in range(CTX)]


def load_rows(refs, extra=0):
    first = 0
    for n, ref in enumerate(refs):
        value = ref[...]
        value = value.reshape(value.shape[-2:])
        if extra and n < 4:
            value = value[extra:]
        yield first, value
        first += value.shape[0]


def row_scale(x):
    return lax.rsqrt(jnp.mean(x * x, axis=-1, keepdims=True) + NORM_EPS)


def project_kernel(count, sp, *refs):
    cw_ref, wc_ref, normed_ref, conv_ref, step_ref = refs[count:]
    gain = cw_ref[8:9, :]
    for first, x in load_rows(refs[:count]):
        x = x.astype(F32)
        rows = pl.ds(first, x.shape[0])
        normed_ref[rows, :] = (x * row_scale(x) * gain).astype(BF16)
    normed = normed_ref[...]
    conv_ref[...] = dot(normed, wc_ref[:, :MIX], AB).astype(BF16)
    step_ref[...] = dot(normed, wc_ref[:, MIX:], AB)


def project(sp, pieces, cw, wc, tokens):
    return call(
        "project",
        functools.partial(project_kernel, len(pieces)),
        sp,
        pieces + [cw, wc],
        [
            shape((tokens, wc.shape[0]), BF16),
            shape((tokens, MIX), BF16),
            shape((tokens, 128), F32),
        ],
    )


def bounds_of(sp):
    return [sp[3 + d] for d in range(sp.shape[0] - 3)]


def distances(sp, first, rows):
    at = lax.broadcasted_iota(jnp.int32, (rows, 1), 0) + first
    since = at
    for bound in bounds_of(sp):
        gap = at - bound
        since = jnp.where(gap >= 0, jnp.minimum(since, gap), since)
    return since


def segment(sp, at):
    total = jnp.zeros_like(at)
    for bound in bounds_of(sp):
        total = total + jnp.where(at >= bound, 1, 0)
    return total


def pair_lanes(a, pair):
    rows = a.shape[0]
    low = lax.broadcasted_iota(jnp.int32, (rows, 2 * HEAD), 1) < HEAD
    first = jnp.broadcast_to(a[:, 2 * pair : 2 * pair + 1], (rows, 2 * HEAD))
    second = jnp.broadcast_to(a[:, 2 * pair + 1 : 2 * pair + 2], (rows, 2 * HEAD))
    return jnp.where(low, first, second)


def conv_forward(ext, cw_ref, since, cols, q):
    total = cw_ref[4:5, cols] + cw_ref[3:4, cols] * ext[8 : 8 + q, cols]
    for shift in range(1, CONV):
        tap = cw_ref[3 - shift : 4 - shift, cols]
        rows = ext[8 - shift : 8 - shift + q, cols]
        total = total + jnp.where(since >= shift, tap * rows, 0.0)
    return total


def block_terms(sp, first, q, raw, cw_ref):
    row = lax.broadcasted_iota(jnp.int32, (q, 1), 0)
    col = lax.broadcasted_iota(jnp.int32, (1, q), 1)
    seg_col, seg_row = segment(sp, row + first), segment(sp, col + first)
    seg_before, seg_last = jnp.int32(0), jnp.int32(0)
    for bound in bounds_of(sp):
        seg_before = seg_before + jnp.where(first - 1 >= bound, 1, 0)
        seg_last = seg_last + jnp.where(first + q - 1 >= bound, 1, 0)
    same = seg_col == seg_row
    shifted = raw + cw_ref[10:11, 0:128]
    stepsize = jax.nn.softplus(shifted)
    decay = -stepsize * cw_ref[11:12, 0:128]
    lower = jnp.where(row >= col, 1.0, 0.0)
    cum = dot(lower, decay, AB, HIGH)
    last = cum[q - 1 : q, :]
    open_w = jnp.where(seg_col == seg_before, jnp.exp(cum), 0.0)
    tail = jnp.where(seg_col == seg_last, jnp.exp(jnp.minimum(last - cum, 0.0)), 0.0)
    passed = jnp.where(seg_last == seg_before, jnp.exp(last), 0.0)
    return row, col, same, shifted, stepsize, decay, cum, open_w, tail, passed


def pair_cols(pair):
    return slice(2 * HEAD * pair, 2 * HEAD * (pair + 1))


def scan_kernel(
    seg,
    sp,
    ci_ref,
    raw_ref,
    cw_ref,
    st_in_ref,
    tail_in_ref,
    y_ref,
    st_ref,
    st_out_ref,
    tail_out_ref,
    ext,
    mix,
    state,
    flow,
    fresh,
):
    k = pl.program_id(0)
    q = ci_ref.shape[0]
    first = (CTX * seg + k) * q

    @pl.when(k == 0)
    def _():
        state[...] = st_in_ref[...]
        ext[0:8, :] = tail_in_ref[...].astype(F32)[8:16, :]

    ci = ci_ref[...]
    tail_out_ref[...] = ci[q - 16 : q, :]
    ext[8 : 8 + q, :] = ci.astype(F32)
    since = distances(sp, first, q)
    for c in range(0, MIX, 128):
        cols = slice(c, c + 128)
        pre = conv_forward(ext, cw_ref, since, cols, q)
        mix[:, cols] = pre * jax.nn.sigmoid(pre)
    ext[0:8, :] = ext[q : q + 8, :]

    row, col, same, _, stepsize, _, cum, open_w, tail, passed = block_terms(
        sp, first, q, raw_ref[...], cw_ref
    )
    cum_t = cum.T
    keys = mix[:, WIDE : WIDE + STATE]
    kt = keys.T.astype(BF16)
    queries = mix[:, WIDE + STATE :]
    qb = queries.astype(BF16)
    scores = jnp.where(same & (row >= col), split_dot(queries, keys, ABT), 0.0)
    st_ref[...] = state[...]
    flow[...] = split_dot(queries, state[...], AB)
    low = lax.broadcasted_iota(jnp.int32, (q, 2 * HEAD), 1) < HEAD
    tail = tail * stepsize
    for pair in range(LOCAL // 2):
        cols = pair_cols(pair)
        v = mix[:, cols]
        vs = v * pair_lanes(stepsize, pair)
        outs = []
        for h in (2 * pair, 2 * pair + 1):
            damp = jnp.exp(jnp.minimum(cum[:, h : h + 1] - cum_t[h : h + 1, :], 0.0))
            outs.append(split_dot(scores * damp, vs, AB))
        inflow = flow[:, cols] * pair_lanes(open_w, pair)
        y = jnp.where(low, outs[0], outs[1]) + inflow + cw_ref[5:6, cols] * v
        y_ref[:, cols] = y
        fresh[:, cols] = (v * pair_lanes(tail, pair)).astype(BF16)
    update = dot(kt, fresh[...], AB)
    for pair in range(LOCAL // 2):
        cols = pair_cols(pair)
        state[:, cols] = state[:, cols] * pair_lanes(passed, pair) + update[:, cols]
    st_out_ref[...] = state[...]


def scan_rows(sp, seg, conv_in, step_raw, cw, state, tail):
    q = conv_in.shape[0] // CTX

    def here(x):
        return x, pl.BlockSpec((q, x.shape[1]), lambda k, sp: (k ^ sp[0], 0))

    tokens = conv_in.shape[0]
    states = pltpu.HBM((CTX * STATE, WIDE), F32)
    return call(
        "scan_rows",
        functools.partial(scan_kernel, seg),
        sp,
        [here(conv_in), here(step_raw), cw, state, tail],
        [
            here(shape((tokens, WIDE), F32)),
            (states, pl.BlockSpec((STATE, WIDE), lambda k, sp: (k, 0))),
            shape((STATE, WIDE), F32),
            shape((16, MIX), BF16),
        ],
        16,
        grid=CTX,
        scratch=[
            pltpu.VMEM((q + 8, MIX), F32),
            pltpu.VMEM((q, MIX), F32),
            pltpu.VMEM((STATE, WIDE), F32),
            pltpu.VMEM((q, WIDE), F32),
            pltpu.VMEM((q, WIDE), BF16),
        ],
    )


def stat_rows(columns):
    rows = columns[0].shape[0]
    lane = lax.broadcasted_iota(jnp.int32, (rows, 128), 1)
    table = jnp.zeros((rows, 128), F32)
    for i, column in enumerate(columns):
        table = jnp.where(lane == i, column, table)
    return table.T[0:8, :]


def stat_columns(rows):
    return jnp.concatenate([rows, jnp.zeros((120, rows.shape[1]), F32)]).T


def split_rows(row, cols):
    high = row.astype(BF16).astype(F32)
    middle = (row - high).astype(BF16).astype(F32)
    low = row - high - middle
    sub = lax.broadcasted_iota(jnp.int32, (16, row.shape[1]), 0)
    tile = jnp.where(sub == 0, high, jnp.where(sub == 1, middle, jnp.where(sub == 2, low, 0.0)))
    spare = jnp.zeros((16, cols - row.shape[1]), F32)
    return jnp.concatenate([tile, spare], axis=1).astype(BF16)


def stat_row(ref, row, count):
    if ref.dtype == F32:
        return ref[row : row + 1, :count]
    tile = ref[...].astype(F32)
    return tile[0:1, :count] + tile[1:2, :count] + tile[2:3, :count]


def store_slots(part, stat, part_refs):
    own_ref, x_ref, y_ref, late_x_ref, late_y_ref = part_refs
    q = own_ref.shape[0]
    half = q // 2
    part = part.astype(BF16)
    own_ref[...] = part[:q]
    x_ref[:half, :] = part[3 * q : 3 * q + half]
    x_ref[half:q, :] = part[q : q + half]
    y_ref[:half, :] = part[3 * q + half :]
    y_ref[half:q, :] = part[2 * q + half : 3 * q]
    late_x_ref[...] = part[q + half : 2 * q]
    late_y_ref[...] = part[2 * q : 2 * q + half]
    if stat is not None:
        tile = split_rows(stat, part.shape[1])
        x_ref[q:, :] = tile
        y_ref[q:, :] = tile


def store_part(part, stat, part_refs):
    if len(part_refs) == 1:
        part_refs[0][...] = part.astype(BF16)
    else:
        store_slots(part, stat, part_refs)


def part_shapes(slots, tokens, d, extra=0):
    if not slots:
        return [shape((tokens, d), BF16)]
    q = tokens // CTX
    sent = shape((q + extra, d), BF16)
    return [shape((q, d), BF16), sent, sent] + [shape((q // 2, d), BF16)] * 2


def tail_tile(x):
    return x, pl.BlockSpec((16, x.shape[1]), lambda i, sp: (x.shape[0] // 16 - 1, 0))


def head_tile(x):
    return x, pl.BlockSpec((16, x.shape[1]), lambda i, sp: (0, 0))


def turn_kernel(sp, from_x_ref, from_y_ref, late_x_ref, late_y_ref, x_ref, y_ref):
    half = y_ref.shape[0]
    x_ref[:half, :] = (late_x_ref[...].astype(F32) + from_y_ref[:half, :].astype(F32)).astype(BF16)
    y_ref[...] = (late_y_ref[...].astype(F32) + from_x_ref[:half, :].astype(F32)).astype(BF16)
    if x_ref.shape[0] > half:
        x_ref[half:, :] = from_y_ref[2 * half :, :]


def out_kernel(count, before, sp, *refs):
    if before:
        before_ref, refs = refs[0], refs[1:]
    normed_ref, y_ref, cw_ref, wg_ref, wo_ref = refs[count : count + 5]
    gate_ref, stat_ref = refs[count + 5 : count + 7]
    gate = dot(normed_ref[...], wg_ref[...], AB)
    gate_ref[...] = gate
    g = y_ref[...] * gate * jax.nn.sigmoid(gate)
    part = dot((g * cw_ref[9:10, :WIDE]).astype(BF16), wo_ref[...], AB)
    square = jnp.sum(g * g, axis=-1, keepdims=True)
    inner = [
        jnp.sum(part[first : first + u.shape[0]] * u.astype(F32), axis=-1, keepdims=True)
        for first, u in load_rows(refs[:count])
    ]
    rows = stat_rows([square] + ([jnp.concatenate(inner)] if inner else []))
    store_part(part, rows[0:1, :], refs[count + 7 :])
    if before:
        rows = jnp.concatenate([before_ref[...], rows])
    stat_ref[...] = rows


def out_rows(sp, slots, before, pieces, normed, y, cw, wg, wo):
    tokens, d = normed.shape
    return call(
        "out_rows",
        functools.partial(out_kernel, len(pieces), len(before)),
        sp,
        before + pieces + [normed, y, cw, wg, wo],
        [shape((tokens, WIDE), F32), shape((8 + 8 * len(before), tokens), F32)] + part_shapes(slots, tokens, d, 16),
        28,
    )


def slot_sums(stat_refs, row, q):
    out = []
    for slot in range(CTX):
        total = 0.0
        for m, ref in enumerate(stat_refs):
            total = total + stat_row(ref, row, CTX * q)[:, (slot ^ m) * q : (slot ^ m) * q + q]
        out.append(total)
    return jnp.concatenate(out, axis=1)


def own_sum(refs):
    own, from_x, from_y, late_x, late_y = [ref[...].astype(F32) for ref in refs]
    half = late_y.shape[0]
    x = jnp.concatenate([from_x[half : 2 * half], late_x[:half]])
    return own + x + jnp.concatenate([late_y, from_y[half : 2 * half]])


def own_squares(stats, sp, natural, q):
    if not natural:
        rows = [stat_row(ref, 0, CTX * q) for ref in stats]
        return sum(row[:, m * q : m * q + q] for m, row in enumerate(rows))
    place, out = sp[0], []
    block = q // 2
    for half in range(2):
        total = jnp.zeros((1, block), F32)
        for s in range(SEGS):
            for slot in range(CTX):
                here = ((place >> 1) == s) & ((slot ^ place) == 2 * (place & 1) + half)
                for m, ref in enumerate(stats):
                    value = ref[8 * s : 8 * s + 1, pl.ds((slot ^ m) * block, block)]
                    total = total + jnp.where(here, value, 0.0)
        out.append(total)
    return jnp.concatenate(out, axis=1)


def own_kernel(count, natural, sp, *refs):
    stats, partial = refs[:CTX], refs[CTX : CTX + 5]
    residual = jnp.concatenate([x for _, x in load_rows(refs[CTX + 5 : CTX + 5 + count])])
    own_ref, branch_ref = refs[CTX + 5 + count :]
    square = own_squares(stats, sp, natural, own_ref.shape[0])
    square = jnp.concatenate([square, jnp.zeros((7, square.shape[1]), F32)])
    scale = lax.rsqrt(stat_columns(square)[:, 0:1] / INNER + NORM_EPS)
    branch = own_sum(partial) * scale
    branch_ref[...] = branch
    own_ref[...] = (residual.astype(F32) + branch).astype(BF16)


def own_rows(sp, natural, stats, partial, residual):
    q, d = partial[0].shape
    return call(
        "own_rows",
        functools.partial(own_kernel, len(residual), natural),
        sp,
        stats + partial + residual,
        [shape((q, d), BF16), shape((q, d), F32)],
        16,
    )


def collect_kernel(sp, part0_ref, part1_ref, own_ref, x_ref, y_ref, late_x_ref, late_y_ref):
    place = sp[0]
    q = late_x_ref.shape[0]
    goals = [
        [own_ref.at[pl.ds(0, q)], own_ref.at[pl.ds(q, q)]],
        [x_ref.at[pl.ds(q, q)], late_x_ref],
        [late_y_ref, y_ref.at[pl.ds(q, q)]],
        [x_ref.at[pl.ds(0, q)], y_ref.at[pl.ds(0, q)]],
    ]
    for m in range(CTX):
        owner = place ^ m
        for half in range(2):
            slot = (2 * (owner & 1) + half) ^ place
            rows = pl.ds(pl.multiple_of(slot * q, q), q)
            goals[m][half][...] = choose((owner >> 1) == 0, part0_ref[rows, :], part1_ref[rows, :])


def collect(sp, parts):
    tokens, d = parts[0].shape
    return call("collect", collect_kernel, sp, list(parts), part_shapes(True, 2 * tokens, d), 20)


def natural_kernel(extra, sp, *refs):
    out_ref = refs[-1]
    q = out_ref.shape[0] // 2
    for place in range(CTX):
        s = place >> 1
        own, x, y, first, second = refs[5 * s : 5 * s + 5]

        @pl.when(sp[0] == place)
        def _():
            for half in range(2):
                slot = (2 * (place & 1) + half) ^ place
                at = half * q
                if slot < 3:
                    out_ref[at : at + q, :] = (own, x, y)[slot][extra:, :]
                else:
                    out_ref[at : at + q // 2, :] = first[extra:, :]
                    out_ref[at + q // 2 : at + q, :] = second[...]


def natural_rows(sp, pieces, extra=0):
    q, d = pieces[0][0].shape
    ins = [x for one in pieces for x in one]
    kernel = functools.partial(natural_kernel, extra)
    return call("natural_rows", kernel, sp, ins, [shape((2 * (q - extra), d), BF16)])[0]


def gate_back_kernel(count, inners, first_stat, sp, *refs):
    pieces, stats = refs[:count], refs[count : count + CTX]
    inner_refs = refs[count + CTX : count + CTX + inners]
    rest = refs[count + CTX + inners :]
    y_ref, gate_ref, cw_ref, wo_ref, dy_ref, dgate_ref, gated_ref, u_ref, dgain_ref = rest
    gain = cw_ref[9:10, :WIDE]
    tokens = y_ref.shape[0]
    q = tokens // CTX
    for first, u in load_rows(pieces, 16 if inners else 0):
        u_ref[pl.ds(first, u.shape[0]), :] = u
    back = dot(u_ref[...], wo_ref[...], ABT)
    scale = lax.rsqrt(slot_sums(stats, first_stat, q) / INNER + NORM_EPS)
    if inners:
        inner = jnp.concatenate([stat_row(ref, 0, q) for ref in inner_refs], axis=1)
    else:
        inner = slot_sums(stats, first_stat + 1, q) * scale
    pull = scale * scale * inner / INNER
    table = stat_columns(jnp.concatenate([scale, pull, jnp.zeros((6, tokens), F32)]))
    scale, pull = table[:, 0:1], table[:, 1:2]
    gate = gate_ref[...]
    y = y_ref[...]
    sig = jax.nn.sigmoid(gate)
    act = gate * sig
    g = y * act
    unit = g * scale
    gated_ref[...] = (unit * gain).astype(BF16)
    dg = back * gain * scale - g * pull
    dy_ref[...] = (dg * act).astype(BF16)
    dgate_ref[...] = (dg * y * (sig + act * (1.0 - sig))).astype(BF16)
    dgain_ref[...] = jnp.broadcast_to(jnp.sum(back * unit, axis=0, keepdims=True), (8, WIDE))


def gate_back(sp, pieces, stats, first_stat, inners, y, gate, cw, wo):
    tokens, d = y.shape[0], wo.shape[1]
    return call(
        "gate_back",
        functools.partial(gate_back_kernel, len(pieces), len(inners), first_stat),
        sp,
        pieces + stats + inners + [y, gate, cw, wo],
        [shape((tokens, WIDE), BF16)] * 3 + [shape((tokens, d), BF16), shape((8, WIDE), F32)],
        28,
    )


def scan_back_kernel(
    seg,
    sp,
    ci_ref,
    prev_ref,
    raw_ref,
    dy_ref,
    st_ref,
    tail_in_ref,
    cw_ref,
    dst_in_ref,
    next_in_ref,
    dci_ref,
    dcw_ref,
    dhp_ref,
    dst_out_ref,
    next_out_ref,
    ext,
    mix,
    slope,
    dext,
    dstate,
    tails,
    dyw,
    flow,
    kept_all,
    ends,
):
    i = pl.program_id(0)
    k = CTX - 1 - i
    q = ci_ref.shape[0]
    first = (CTX * seg + k) * q

    @pl.when(i == 0)
    def _():
        dstate[...] = dst_in_ref[...]
        dext[q : q + 8, :] = next_in_ref[...]
        ends[...] = jnp.zeros_like(ends)
        dcw_ref[...] = jnp.zeros_like(dcw_ref)
        dhp_ref[...] = jnp.zeros_like(dhp_ref)

    @pl.when(k == 0)
    def _():
        ext[0:8, :] = tail_in_ref[...].astype(F32)[8:16, :]

    @pl.when(k > 0)
    def _():
        ext[0:8, :] = prev_ref[...].astype(F32)[8:16, :]

    ext[8 : 8 + q, :] = ci_ref[...].astype(F32)
    since = distances(sp, first, q + 8)
    for c in range(0, MIX, 128):
        cols = slice(c, c + 128)
        pre = conv_forward(ext, cw_ref, since[0:q], cols, q)
        sig = jax.nn.sigmoid(pre)
        act = pre * sig
        mix[:, cols] = act
        slope[:, cols] = sig + act * (1.0 - sig)

    row, col, same, shifted, stepsize, decay, cum, open_w, tail, passed = block_terms(
        sp, first, q, raw_ref[...], cw_ref
    )
    cum_t = cum.T
    keys = mix[:, WIDE : WIDE + STATE]
    kb = keys.astype(BF16)
    queries = mix[:, WIDE + STATE :]
    qb = queries.astype(BF16)
    qt = queries.T.astype(BF16)
    inside = same & (col >= row)
    scores = jnp.where(inside, split_dot(keys, queries, ABT), 0.0)
    stb, dstb = st_ref[...].astype(BF16), dstate[...].astype(BF16)
    flow[...] = dot(qb, stb, AB)
    kept_all[...] = dot(kb, dstb, AB)
    low = lax.broadcasted_iota(jnp.int32, (q, 2 * HEAD), 1) < HEAD
    lane = lax.broadcasted_iota(jnp.int32, (q, 128), 1)
    sub = lax.broadcasted_iota(jnp.int32, (16, q), 0)
    dscores = jnp.zeros((q, q), F32)
    plus_t = jnp.zeros((16, q), F32)
    dstep = jnp.zeros((q, 128), F32)
    dcum = jnp.zeros((q, 128), F32)
    for pair in range(LOCAL // 2):
        cols = pair_cols(pair)
        v = mix[:, cols]
        step_e = pair_lanes(stepsize, pair)
        vs = v * step_e
        vsb = vs.astype(BF16)
        dyb = dy_ref[:, cols]
        dyf = dyb.astype(F32)
        dvs = []
        for side, h in ((0, 2 * pair), (1, 2 * pair + 1)):
            mine = low if side == 0 else ~low
            damp = jnp.exp(jnp.minimum(cum_t[h : h + 1, :] - cum[:, h : h + 1], 0.0))
            raw = dot(jnp.where(mine, vs, 0.0).astype(BF16), dyb, ABT)
            mixing = (scores * damp).astype(BF16)
            dscores = dscores + raw * damp
            both = raw * mixing.astype(F32)
            plus_t = plus_t + jnp.where(sub == h, jnp.sum(both, axis=0, keepdims=True), 0.0)
            dvs.append(dot(mixing, dyb, AB))
        dv = jnp.where(low, dvs[0], dvs[1])
        weighted = dyf * pair_lanes(open_w, pair)
        dyw[:, cols] = weighted.astype(BF16)
        tail_e = pair_lanes(tail, pair)
        kept = kept_all[:, cols] * tail_e
        tails[:, cols] = (vs * tail_e).astype(BF16)
        u = dv + kept
        dext[0:q, cols] = (u * step_e + cw_ref[5:6, cols] * dyf) * slope[:, cols]
        from_tail = kept * vs
        dcw_ref[5:6, cols] += jnp.sum(dyf * v, axis=0, keepdims=True)
        ends[1:2, cols] = jnp.sum(from_tail, axis=0, keepdims=True)
        uv = u * v
        change = weighted * flow[:, cols] - dv * vsb.astype(F32) - from_tail
        for side, h in ((0, 2 * pair), (1, 2 * pair + 1)):
            mine = low if side == 0 else ~low

            def per_row(x):
                return jnp.sum(jnp.where(mine, x, 0.0), axis=1, keepdims=True)

            dstep = jnp.where(lane == h, per_row(uv), dstep)
            dcum = jnp.where(lane == h, per_row(change), dcum)

    dcum = dcum + jnp.concatenate([plus_t, jnp.zeros((112, q), F32)]).T
    ends[0:1, :] = jnp.sum(st_ref[...] * dstate[...], axis=0, keepdims=True)
    by_head = dot(ends[...], channel_map(), AB, HIGH)
    at_end = by_head[0:1, :] * passed + by_head[1:2, :]
    dcum = dcum + jnp.where(row == q - 1, at_end, 0.0)
    upper = jnp.where(col >= row, 1.0, 0.0)
    ddecay = dot(upper, dcum, AB, HIGH)
    draw = (dstep - ddecay * cw_ref[11:12, 0:128]) * jax.nn.sigmoid(shifted)
    dci_ref[:, MIX:] = draw.astype(BF16)
    dhp_ref[0:1, :] += jnp.sum(draw, axis=0, keepdims=True)
    dhp_ref[1:2, :] += jnp.sum(ddecay * decay, axis=0, keepdims=True)

    dsb = jnp.where(inside, dscores, 0.0).astype(BF16)
    dkeys = dot(dsb, qb, AB) + dot(tails[...], dstb, ABT)
    dqueries = dot(dsb, kb, ATB) + dot(dyw[...], stb, ABT)
    kcols, qcols = slice(WIDE, WIDE + STATE), slice(WIDE + STATE, MIX)
    dext[0:q, kcols] = dkeys * slope[:, kcols]
    dext[0:q, qcols] = dqueries * slope[:, qcols]
    update = dot(qt, dyw[...], AB)
    for pair in range(LOCAL // 2):
        cols = pair_cols(pair)
        dstate[:, cols] = dstate[:, cols] * pair_lanes(passed, pair) + update[:, cols]
    dst_out_ref[...] = dstate[...]

    for c in range(0, MIX, 128):
        cols = slice(c, c + 128)
        here = dext[0:q, cols]
        total = cw_ref[3:4, cols] * here
        dcw_ref[3:4, cols] += jnp.sum(here * ext[8 : 8 + q, cols], axis=0, keepdims=True)
        dcw_ref[4:5, cols] += jnp.sum(here, axis=0, keepdims=True)
        for shift in range(1, CONV):
            later = jnp.where(since[shift : shift + q] >= shift, dext[shift : shift + q, cols], 0.0)
            total = total + cw_ref[3 - shift : 4 - shift, cols] * later
            used = jnp.where(since[0:q] >= shift, ext[8 - shift : 8 - shift + q, cols], 0.0)
            dcw_ref[3 - shift : 4 - shift, cols] += jnp.sum(here * used, axis=0, keepdims=True)
        dci_ref[:, cols] = total.astype(BF16)
    head_rows = dext[0:8, :]
    dext[q : q + 8, :] = head_rows
    next_out_ref[...] = head_rows


def scan_back(sp, stored, seg, conv_in, step_raw, dy, states, tail, cw, dstate, following):
    tokens = conv_in.shape[0]
    q = tokens // CTX

    def here(x):
        return x, pl.BlockSpec((q, x.shape[1]), lambda i, sp: ((CTX - 1 - i) ^ sp[0], 0))

    if stored:
        conv_in, step_raw, dy, states = [far(x) for x in (conv_in, step_raw, dy, states)]
        tail, cw, dstate, following = [far(x) for x in (tail, cw, dstate, following)]

    def before(i, sp):
        return (jnp.maximum(CTX - 2 - i, 0) ^ sp[0]) * (q // 16) + q // 16 - 1, 0

    return call(
        "scan_back",
        functools.partial(scan_back_kernel, seg),
        sp,
        [
            here(conv_in),
            (conv_in, pl.BlockSpec((16, MIX), before)),
            here(step_raw),
            here(dy),
            (states, pl.BlockSpec((STATE, WIDE), lambda i, sp: (CTX - 1 - i, 0))),
            tail,
            cw,
            dstate,
            following,
        ],
        [
            here(shape((tokens, FULL), BF16)),
            shape((8, MIX), F32),
            shape((8, 128), F32),
            shape((STATE, WIDE), F32),
            shape((8, MIX), F32),
        ],
        24,
        grid=CTX,
        scratch=[
            pltpu.VMEM((q + 8, MIX), F32),
            pltpu.VMEM((q, MIX), F32),
            pltpu.VMEM((q, MIX), F32),
            pltpu.VMEM((q + 8, MIX), F32),
            pltpu.VMEM((STATE, WIDE), F32),
            pltpu.VMEM((q, WIDE), BF16),
            pltpu.VMEM((q, WIDE), BF16),
            pltpu.VMEM((q, WIDE), F32),
            pltpu.VMEM((q, WIDE), F32),
            pltpu.VMEM((8, WIDE), F32),
        ],
    )


def input_back_kernel(sp, dc_ref, dg_ref, wc_ref, wg_ref, *part_refs):
    part = dot(dc_ref[...], wc_ref[...], ABT) + dot(dg_ref[...], wg_ref[...], ABT)
    store_part(part, None, part_refs)


def input_back(sp, slots, dconv, dgate, wc, wg):
    outs = part_shapes(slots, dconv.shape[0], wc.shape[0])
    return call("input_back", input_back_kernel, sp, [dconv, dgate, wc, wg], outs, 24)


def own_back_kernel(count, sp, *refs):
    partial, rest = refs[:5], refs[5:]
    x = jnp.concatenate([v for _, v in load_rows(rest[:count])]).astype(F32)
    u = jnp.concatenate([v for _, v in load_rows(rest[count : 2 * count])]).astype(F32)
    cw_ref, branch_ref, up_ref, dnorm_ref = rest[2 * count :]
    grad = own_sum(partial)
    scale = row_scale(x)
    gained = grad * cw_ref[8:9, :]
    centre = jnp.mean(gained * x, axis=-1, keepdims=True)
    up = (u + scale * (gained - x * (scale * scale * centre))).astype(BF16)
    extra = up_ref.shape[0] - up.shape[0]
    up_ref[extra:, :] = up
    if extra:
        inner = jnp.sum(up.astype(F32) * branch_ref[...], axis=-1, keepdims=True)
        up_ref[:extra, :] = split_rows(stat_rows([inner])[0:1, :], up.shape[1])
    dnorm_ref[...] = jnp.broadcast_to(
        jnp.sum(grad * x * scale, axis=0, keepdims=True), dnorm_ref.shape
    )


def own_back(sp, extra, partial, x, u, cw, branch):
    q, d = partial[0].shape
    return call(
        "own_back",
        functools.partial(own_back_kernel, len(x)),
        sp,
        partial + x + u + [cw, branch],
        [shape((q + extra, d), BF16), shape((8, d), F32)],
    )


def head_map(group, block, flipped=False):
    here = lax.broadcasted_iota(jnp.int32, (128, 128), 1 if flipped else 0)
    there = lax.broadcasted_iota(jnp.int32, (128, 128), 0 if flipped else 1)
    turn = jnp.zeros_like(here)
    for edge in range(block, LOCAL, block):
        turn = turn + jnp.where(here >= edge, 1, 0)
    goal = here + (turn * (CTX - 1) + group) * block
    return jnp.where((here < LOCAL) & (there == goal), 1.0, 0.0)


def channel_map(flipped=False):
    dims = (128, WIDE) if flipped else (WIDE, 128)
    chan = lax.broadcasted_iota(jnp.int32, dims, 1 if flipped else 0)
    head = lax.broadcasted_iota(jnp.int32, dims, 0 if flipped else 1)
    return jnp.where((chan >= head * HEAD) & (chan < (head + 1) * HEAD), 1.0, 0.0)


def spans(group, block):
    wide = block * HEAD
    return [(z * wide, (z * CTX + group) * wide, wide) for z in range(WIDE // wide)]


def choose(first, a, b):
    return jnp.where(first, a, b)


def pack_kernel(block, sp, w_ref, *refs):
    conv_refs, gate_refs, conv, gate = refs[:CTX], refs[CTX : 2 * CTX], refs[-2], refs[-1]
    place = sp[0]
    keys = w_ref[:, 2 * INNER : 2 * INNER + STATE]
    queries = w_ref[:, 2 * INNER + STATE : 2 * INNER + 2 * STATE]
    steps = w_ref[:, 2 * INNER + 2 * STATE :]
    rows = w_ref.shape[0]
    steps = jnp.concatenate([steps, jnp.zeros((rows, 128 - HEADS), BF16)], axis=1)
    for k in range(CTX):
        values = jnp.concatenate(
            [w_ref[:, INNER + there : INNER + there + n] for _, there, n in spans(k, block)], axis=1
        )
        gates = jnp.concatenate(
            [w_ref[:, there : there + n] for _, there, n in spans(k, block)], axis=1
        )
        step = dot(steps, head_map(k, block, True).astype(BF16), AB).astype(BF16)
        conv[k] = jnp.concatenate(
            [values[:, :HALF], keys, step, values[:, HALF:], queries, step], axis=1
        )
        gate[k] = gates
    for m in range(CTX):
        conv_refs[m][...] = conv[m ^ place]
        gate_refs[m][...] = gate[m ^ place]


def pack(sp, block, w_in):
    rows = w_in.shape[0]
    outs = call(
        "pack",
        functools.partial(pack_kernel, block),
        sp,
        [w_in],
        [shape((rows, 2 * LOAD), BF16)] * CTX + [shape((rows, WIDE), BF16)] * CTX,
        16,
        scratch=[
            pltpu.VMEM((CTX, rows, 2 * LOAD), BF16),
            pltpu.VMEM((CTX, rows, WIDE), BF16),
        ],
    )
    return outs[:CTX], outs[CTX:]


def order_conv_kernel(sp, *refs):
    keep_ref, send_ref = refs[CTX:]
    zero = sp[1] == 0
    for m in range(CTX):
        low, high = refs[m][:, :LOAD], refs[m][:, LOAD:]
        keep_ref[m ^ sp[0]] = choose(zero, low, high)
        send_ref[m ^ sp[0]] = choose(zero, high, low)


def order_conv(sp, slots):
    out = shape((CTX, slots[0].shape[0], LOAD), BF16)
    return call("order_conv", order_conv_kernel, sp, slots, [out, out], 12)


def order_gate_kernel(sp, *refs):
    out_ref, keep_ref, send_ref = refs[CTX:]
    zero = sp[1] == 0
    rows = keep_ref.shape[1]
    for m in range(CTX):
        low, high = refs[m][:, :HALF], refs[m][:, HALF:]
        keep_ref[m ^ sp[0], :, :HALF] = choose(zero, low, high)
        send_ref[m ^ sp[0], :, :HALF] = choose(zero, high, low)
    for r in range(2):
        for c in range(2):
            at = slice(r * rows, (r + 1) * rows)
            low = out_ref[at, c * HALF : (c + 1) * HALF]
            high = out_ref[at, (2 + c) * HALF : (3 + c) * HALF]
            keep_ref[2 * r + c, :, HALF:] = choose(zero, low, high)
            send_ref[2 * r + c, :, HALF:] = choose(zero, high, low)


def order_gate(sp, slots, w_out):
    out = shape((CTX, slots[0].shape[0], WIDE), BF16)
    return call("order_gate", order_gate_kernel, sp, slots + [w_out], [out, out], 12)


def join_conv_kernel(sp, mine_ref, other_ref, wc_ref):
    zero = sp[1] == 0
    rows = mine_ref.shape[2]
    for i in range(CTX):
        a, b = mine_ref[0, i, :, :LOAD], other_ref[0, i, :, :LOAD]
        low, high = choose(zero, a, b), choose(zero, b, a)
        at = slice(i * rows, (i + 1) * rows)
        wc_ref[at, 0:HALF] = low[:, :HALF]
        wc_ref[at, HALF:WIDE] = high[:, :HALF]
        wc_ref[at, WIDE : WIDE + STATE] = low[:, HALF : HALF + STATE]
        wc_ref[at, WIDE + STATE : MIX] = high[:, HALF : HALF + STATE]
        wc_ref[at, MIX:] = low[:, HALF + STATE :]


def by_rows(x, count):
    return x, pl.BlockSpec((x.shape[0] // count, x.shape[1]), lambda z, sp: (z, 0))


def join_conv(sp, mine, other):
    dp, _, rows, _ = mine.shape
    out = by_rows(shape((dp * CTX * rows, FULL), BF16), dp)
    ins = [by_first(mine), by_first(other)]
    return call("join_conv", join_conv_kernel, sp, ins, [out], 12, dp)[0]


def join_gate_kernel(first, sp, mine_ref, other_ref, wg_ref, wo_ref):
    zero = sp[1] == 0
    rows = mine_ref.shape[2]
    for i in range(CTX):
        a, b = mine_ref[0, i, :, first:], other_ref[0, i, :, first:]
        low, high = choose(zero, a, b), choose(zero, b, a)
        at = slice(i * rows, (i + 1) * rows)
        wg_ref[at, :HALF] = low[:, :HALF]
        wg_ref[at, HALF:] = high[:, :HALF]
        r, c = i // 2, i % 2
        at = slice(r * rows, (r + 1) * rows)
        wo_ref[at, c * HALF : (c + 1) * HALF] = low[:, HALF:]
        wo_ref[at, (2 + c) * HALF : (3 + c) * HALF] = high[:, HALF:]


def join_gate(sp, mine, other):
    dp, _, rows, cols = mine.shape
    wg, wo = shape((dp * CTX * rows, WIDE), BF16), shape((dp * 2 * rows, 4 * HALF), BF16)
    outs = [by_rows(wg, dp), by_rows(wo, dp)]
    kernel = functools.partial(join_gate_kernel, cols - WIDE)
    ins = [by_first(mine), by_first(other)]
    return call("join_gate", kernel, sp, ins, outs, 12, dp)


def fold_kernel(sp, keep_ref, came_ref, out_ref):
    out_ref[...] = (keep_ref[...].astype(F32) + came_ref[...].astype(F32)).astype(BF16)


def fold(sp, keep, came):
    ins = [by_first(keep), by_first(came)]
    return call("fold", fold_kernel, sp, ins, [by_first(shape(keep.shape, BF16))], 24, keep.shape[0])


def total_kernel(counts, sp, *refs):
    for m in range(CTX):
        parts = [ref[m ^ sp[0], :, :cols] for ref, cols in zip(refs, counts)]
        refs[len(counts) + m][...] = jnp.concatenate(parts, axis=1)


def total_line(sp, sums):
    width = {LOAD: LOAD, WIDE: HALF}
    counts = [width[x.shape[2]] for x in sums]
    outs = [shape((sums[0].shape[1], sum(counts)), BF16)] * CTX
    sums = [far(x) for x in sums]
    return call("total_line", functools.partial(total_kernel, counts), sp, sums, outs)


def mix_kernel(cols, sp, *refs):
    out_ref = refs[-1]
    zero = sp[1] == 0
    for m in range(CTX):
        if cols == LOAD:
            mine, other = refs[CTX + m][...], refs[m][:, :LOAD]
        else:
            mine, other = refs[m][:, LOAD + HALF :], refs[m][:, LOAD : LOAD + HALF]
            out_ref[m, :, HALF:] = choose(zero, refs[CTX + 1][m, :, HALF:], refs[CTX][m, :, HALF:])
        out_ref[m, :, : mine.shape[1]] = choose(zero, other, mine)


def mix(sp, early, late, cols):
    out = shape((CTX, early[0].shape[0], cols), BF16)
    return call("mix", functools.partial(mix_kernel, cols), sp, early + late, [out])[0]


def grad_conv_kernel(sp, n0_ref, n1_ref, d0_ref, d1_ref, keep_ref, send_ref):
    zero = sp[1] == 0
    rows = keep_ref.shape[2]
    total = dot(n0_ref[...], d0_ref[...], ATB) + dot(n1_ref[...], d1_ref[...], ATB)
    total = total.astype(BF16)
    step = total[:, MIX:]
    low = jnp.concatenate([total[:, :HALF], total[:, WIDE : WIDE + STATE], step], axis=1)
    high = jnp.concatenate([total[:, HALF:WIDE], total[:, WIDE + STATE : MIX], step], axis=1)
    keep, send = choose(zero, low, high), choose(zero, high, low)
    for i in range(CTX):
        keep_ref[0, i] = keep[i * rows : (i + 1) * rows]
        send_ref[0, i] = send[i * rows : (i + 1) * rows]


def by_first(x):
    rest = (0,) * (len(x.shape) - 1)
    return x, pl.BlockSpec((1,) + tuple(x.shape[1:]), lambda z, sp: (z,) + rest)


def by_cols(x, count):
    return x, pl.BlockSpec((x.shape[0], x.shape[1] // count), lambda z, sp: (0, z))


def grad_conv(sp, dp, rows, normed, dconv):
    out = shape((dp, CTX, rows, LOAD), BF16)
    return call(
        "grad_conv",
        grad_conv_kernel,
        sp,
        [by_cols(x, dp) for x in normed] + list(dconv),
        [by_first(out), by_first(out)],
        24,
        dp,
    )


def grad_gate_kernel(sp, *refs):
    n_refs, dg_refs, gated_refs, u_refs = refs[0:2], refs[2:4], refs[4:6], refs[6:8]
    keep_ref, send_ref = refs[8:]
    z = pl.program_id(0)
    dp, _, rows, _ = keep_ref.shape
    zero = sp[1] == 0

    def over_tokens(a, b):
        return dot(a[0][...], b[0][...], ATB) + dot(a[1][...], b[1][...], ATB)

    total = over_tokens(n_refs, dg_refs).astype(BF16)
    keep = choose(zero, total[:, :HALF], total[:, HALF:])
    send = choose(zero, total[:, HALF:], total[:, :HALF])
    for i in range(CTX):
        keep_ref[z, i, :, :HALF] = keep[i * rows : (i + 1) * rows]
        send_ref[z, i, :, :HALF] = send[i * rows : (i + 1) * rows]
    total = over_tokens(gated_refs, u_refs).astype(BF16)
    side, c = z // 2, lax.rem(z, 2)

    def put(ref):
        for there in range(dp):
            for r in range(2):
                first = (2 * there + r) * rows
                ref[there, 2 * r + c, :, HALF:] = total[first : first + rows]

    @pl.when(side == sp[1])
    def _():
        put(keep_ref)

    @pl.when(side != sp[1])
    def _():
        put(send_ref)


def grad_gate(sp, dp, rows, normed, dgate, gated, u):
    out = shape((dp, CTX, rows, WIDE), BF16)
    return call(
        "grad_gate",
        grad_gate_kernel,
        sp,
        [by_cols(x, dp) for x in normed]
        + list(dgate)
        + list(gated)
        + [by_cols(x, dp) for x in u],
        [out, out],
        32,
        dp,
    )


def finish_kernel(block, sp, *refs):
    early, late, (gate0, gate1, came_gate, came_conv) = refs[:4], refs[4:8], refs[8:12]
    in_ref, out_ref, lows, highs, glows, ghighs = refs[12:]
    place, zero = sp[0], sp[1] == 0
    rows = in_ref.shape[0]
    for m in range(CTX):
        mine, came = choose(zero, late[m][...], early[m][:, :LOAD]), came_conv[m]
        lows[m ^ place] = choose(zero, mine, came).astype(F32)
        highs[m ^ place] = choose(zero, came, mine).astype(F32)
        mine = choose(zero, early[m][:, LOAD + HALF :], early[m][:, LOAD : LOAD + HALF])
        came = came_gate[m, :, :HALF]
        glows[m ^ place] = choose(zero, mine, came).astype(F32)
        ghighs[m ^ place] = choose(zero, came, mine).astype(F32)
    keys, queries, steps = 0.0, 0.0, 0.0
    for k in range(CTX):
        keys = keys + lows[k, :, HALF : HALF + STATE]
        queries = queries + highs[k, :, HALF : HALF + STATE]
        steps = steps + dot(lows[k, :, HALF + STATE :], head_map(k, block), AB, HIGH)
    for z in range(WIDE // (block * HEAD)):
        def side_by_side(a, b):
            parts = []
            for k in range(CTX):
                here, _, n = spans(k, block)[z]
                source = a if here < HALF else b
                parts.append(source[k, :, here % HALF : here % HALF + n])
            return jnp.concatenate(parts, axis=1)

        wide = CTX * block * HEAD
        in_ref[:, z * wide : (z + 1) * wide] = side_by_side(glows, ghighs)
        in_ref[:, INNER + z * wide : INNER + (z + 1) * wide] = side_by_side(lows, highs)
    in_ref[:, 2 * INNER : 2 * INNER + STATE] = keys
    in_ref[:, 2 * INNER + STATE : 2 * INNER + 2 * STATE] = queries
    in_ref[:, 2 * INNER + 2 * STATE :] = steps[:, :HEADS]
    for i in range(4):
        r, c = i // 2, i % 2
        mine, came = choose(zero, gate0[i, :, HALF:], gate1[i, :, HALF:]), came_gate[i, :, HALF:]
        at = slice(r * rows, (r + 1) * rows)
        out_ref[at, c * HALF : (c + 1) * HALF] = choose(zero, mine, came).astype(F32)
        out_ref[at, (2 + c) * HALF : (3 + c) * HALF] = choose(zero, came, mine).astype(F32)


def finish(sp, block, early, late, gates, came_gate, came_conv):
    rows = came_conv.shape[1]
    return call(
        "finish",
        functools.partial(finish_kernel, block),
        sp,
        early + late + gates + [came_gate, came_conv],
        [shape((rows, 2 * INNER + 2 * STATE + HEADS), F32), shape((2 * rows, 4 * HALF), F32)],
        24,
        scratch=[pltpu.VMEM((CTX, rows, LOAD), F32)] * 2 + [pltpu.VMEM((CTX, rows, HALF), F32)] * 2,
    )


class Direct:
    def __init__(self, order, mine, dp, block, w_in, w_out):
        self.order, self.mine, self.dp, self.block = order, mine, dp, block
        self.rows = w_in.shape[0]
        conv, gate = order(pack, block, w_in)
        conv = order(order_conv, [flip(x, m) if m else x for m, x in enumerate(conv)])
        self.conv = self.trade(*conv)
        self.first = self.gathered(self.conv[0])
        gate = [order.now(x) for x in gate]
        self.slots = [flip(x, m) if m else x for m, x in enumerate(gate)]
        self.w_out = w_out

    def prepare_gate(self):
        self.gate = self.trade(*self.order(order_gate, self.slots, self.w_out))

    def trade(self, keep, send):
        came = swap_core(send)
        return choose(self.mine == 0, keep, came), choose(self.mine == 0, came, keep)

    def gathered(self, x):
        return lax.all_gather(x, "dp", axis=0)

    def start_conv(self):
        return self.first

    def start_gate(self, after):
        x, _ = lax.optimization_barrier((self.order.now(self.gate[0]), after))
        return self.gathered(x)

    def start_second(self):
        return self.gathered(self.order.now(self.conv[1])), self.gathered(self.order.now(self.gate[1]))

    def trade_weights(self, x):
        x = self.order.now(x)
        return x, swap_core(x)

    def conv_weights(self, sp, both):
        return join_conv(sp, *both)

    def gate_weights(self, sp, both):
        return join_gate(sp, *both)

    def grad_gate(self, sp, layer, normed, dgate, gated, u):
        return grad_gate(sp, self.dp, self.rows, normed, dgate, gated, u)

    def grad_conv(self, sp, layer, normed, dconv):
        return grad_conv(sp, self.dp, self.rows, normed, dconv)

    def trade_grads(self, grads):
        return grads[0], swap_core(grads[1])

    def send(self, traded):
        (total,) = self.order(fold, *traded)
        return lax.psum_scatter(total, "dp", scatter_dimension=0, tiled=True)[0]

    def early(self, conv1, gate1, gate0):
        self.gates = [gate0, gate1]
        slots = self.order(total_line, [conv1, gate1, gate0])
        self.slots = [flip(x, m) if m else x for m, x in enumerate(slots)]

    def early_trade(self):
        self.came = swap_core(self.order(mix, self.slots, self.gates, WIDE))

    def late(self, conv0):
        late = self.order(total_line, [conv0])
        self.last = [flip(x, m) if m else x for m, x in enumerate(late)]

    def late_trade(self):
        self.last_came = swap_core(self.order(mix, self.slots, self.last, LOAD))

    def gradients(self):
        arrays = self.slots, self.last, self.gates, self.came, self.last_came
        return self.order(finish, self.block, *arrays)


def grouped(columns, block):
    lead = columns.shape[:-1]
    split = jnp.moveaxis(columns.reshape(lead + (-1, CTX, block)), -2, 0)
    return split.reshape((CTX,) + lead + (-1,))


def ungrouped(groups, block):
    lead = groups.shape[1:-1]
    split = groups.reshape((CTX,) + lead + (-1, block))
    return jnp.moveaxis(split, 0, -2).reshape(lead + (-1,))


def pad_to(x, rows, cols):
    room = [(0, 0)] * (x.ndim - 2) + [(0, rows - x.shape[-2]), (0, cols - x.shape[-1])]
    return jnp.pad(x, room)


class Plain:
    def __init__(self, mine, place, block, w_in, w_out):
        self.mine, self.place, self.block = mine, place, block
        full_in = lax.all_gather(w_in, ("dp", "ctx"), axis=0, tiled=True)
        full_out = lax.all_gather(w_out, ("dp", "ctx"), axis=0, tiled=True)
        self.full = [(full_in, full_out), (swap_core(full_in), swap_core(full_out))]
        self.grads = [{}, {}]

    def prepare_gate(self):
        pass

    def start_conv(self):
        return 0

    def start_gate(self, after):
        return 0

    def start_second(self):
        return 1, 1

    def trade_weights(self, layer):
        return layer

    def trade_grads(self, grads):
        return grads

    def send(self, traded):
        return traded

    def early(self, conv1, gate1, gate0):
        pass

    def early_trade(self):
        pass

    def late(self, conv0):
        pass

    def late_trade(self):
        pass

    def group(self, columns, block):
        return lax.dynamic_index_in_dim(grouped(columns, block), self.place, 0, False)

    def layer(self, layer, which):
        return choose(self.mine == layer, self.full[0][which], self.full[1][which])

    def conv_weights(self, sp, layer):
        one = self.layer(layer, 0)
        values = self.group(one[:, INNER : 2 * INNER], self.block * HEAD)
        step = self.group(one[:, 2 * INNER + 2 * STATE :], self.block)
        shared = one[:, 2 * INNER : 2 * INNER + 2 * STATE]
        return jnp.concatenate([values, shared, pad_to(step, step.shape[0], 128)], 1)

    def gate_weights(self, sp, layer):
        one, out = self.layer(layer, 0), self.layer(layer, 1)
        wide = self.block * HEAD
        return self.group(one[:, :INNER], wide), self.group(out.T, wide).T

    def over_tokens(self, a, b):
        both = [dot(x, y, ATB) for x, y in zip(a, b)]
        return (both[0] + both[1]).astype(BF16)

    def grad_gate(self, sp, layer, normed, dgate, gated, u):
        out = self.over_tokens(gated, u)
        self.grads[layer].update(gate=self.over_tokens(normed, dgate), out=out)
        return [out]

    def grad_conv(self, sp, layer, normed, dconv):
        self.grads[layer].update(conv=self.over_tokens(normed, dconv))
        return [self.grads[layer]["conv"]]

    def spread(self, columns, block):
        at = lax.broadcasted_iota(jnp.int32, (CTX, 1, 1), 0) == self.place
        return ungrouped(jnp.where(at, columns[None], jnp.zeros((), columns.dtype)), block)

    def gradients(self):
        wide = self.block * HEAD
        fulls = []
        for grads in self.grads:
            gate, conv = grads["gate"], grads["conv"]
            grad_in = jnp.concatenate(
                [
                    self.spread(gate, wide),
                    self.spread(conv[:, :WIDE], wide),
                    conv[:, WIDE:MIX],
                    self.spread(conv[:, MIX : MIX + LOCAL], self.block),
                ],
                -1,
            )
            fulls.append((grad_in, self.spread(grads["out"].T, wide).T))
        sums = []
        for a, b in zip(*fulls):
            zero = self.mine == 0
            total = choose(zero, a, b).astype(F32) + swap_core(choose(zero, b, a)).astype(F32)
            total = total.astype(BF16)
            sums.append(
                lax.psum_scatter(total, ("dp", "ctx"), scatter_dimension=0, tiled=True).astype(F32)
            )
        return sums[0], sums[1]


def prepare_kernel(block, sp, norm_ref, taps_ref, bias_ref, dt_ref, log_ref, skip_ref, gain_ref, out_ref):
    out_ref[...] = jnp.zeros_like(out_ref)
    for k in range(CTX):

        @pl.when(sp[0] == k)
        def _():
            for here, there, n in spans(k, block):
                out_ref[0:CONV, here : here + n] = taps_ref[0, :, there : there + n]
                out_ref[4:5, here : here + n] = bias_ref[:, there : there + n]
                out_ref[9:10, here : here + n] = gain_ref[:, there : there + n]
            spare = jnp.zeros((1, 128 - HEADS), F32)
            rows = [jnp.concatenate([ref[...], spare], axis=1) for ref in (dt_ref, log_ref, skip_ref)]
            rows = jnp.concatenate(rows + [jnp.zeros((5, 128), F32)])
            local = dot(rows, head_map(k, block, True), AB, HIGH)
            out_ref[10:11, 0:128] = local[0:1, :]
            out_ref[11:12, 0:128] = jnp.exp(local[1:2, :])
            out_ref[5:6, :WIDE] = dot(local, channel_map(True), AB, HIGH)[2:3, :]

    out_ref[0:CONV, WIDE:MIX] = taps_ref[0, :, INNER:]
    out_ref[4:5, WIDE:MIX] = bias_ref[:, INNER:]
    out_ref[8:9, :] = norm_ref[...]


def prepare(sp, block, arrays):
    out = shape((16, arrays[0].shape[1]), F32)
    return call("prepare", functools.partial(prepare_kernel, block), sp, arrays, [out], 12)[0]


def gather_small_kernel(counts, sp, *refs):
    keep_ref, send_ref = refs[-2:]
    packed, at = [], 0
    for layer in range(2):
        sums = []
        for count in counts[layer]:
            sums.append(sum(ref[...] for ref in refs[at : at + count]))
            at += count
        dcw, dhp, dgain, dnorm = sums
        tall = lax.broadcasted_iota(jnp.int32, (8, MIX), 0)
        gain = jnp.concatenate([dgain, jnp.zeros((8, MIX - WIDE), F32)], axis=1)
        short = dnorm.shape[1] - MIX
        norm_rest = jnp.concatenate([dnorm[:, MIX:], jnp.zeros((8, MIX - short), F32)], axis=1)
        middle = jnp.where(tall == 0, gain, jnp.where(tall == 1, dnorm[:, :MIX], norm_rest))
        heads = jnp.concatenate([dhp, jnp.zeros((8, MIX - 128), F32)], axis=1)
        packed.append(jnp.concatenate([dcw, middle, heads]))
    zero = sp[1] == 0
    keep_ref[...] = choose(zero, packed[0], packed[1])
    send_ref[...] = choose(zero, packed[1], packed[0])


def gather_small(sp, small):
    counts = [[len(kind) for kind in layer] for layer in small]
    arrays = [x for layer in small for kind in layer for x in kind]
    out = shape((PACK, MIX), F32)
    kernel = functools.partial(gather_small_kernel, counts)
    return call("gather_small", kernel, sp, arrays, [out, out], 12)


def spread_small_kernel(block, sp, *refs):
    slots, all_slots = refs[:CTX], refs[-1]
    norm_ref, taps_ref, bias_ref, dt_ref, log_ref, skip_ref, gain_ref = refs[CTX:-1]
    for m in range(CTX):
        all_slots[m ^ sp[0]] = slots[m][...]
    total = sum(all_slots[k] for k in range(CTX))
    norm_ref[:, :MIX] = total[9:10, :]
    norm_ref[:, MIX:] = total[10:11, : norm_ref.shape[1] - MIX]
    taps_ref[0, :, INNER:] = total[0:CONV, WIDE:]
    bias_ref[:, INNER:] = total[4:5, WIDE:]
    pick = channel_map()
    heads = 0.0
    for k in range(CTX):
        for here, there, n in spans(k, block):
            taps_ref[0, :, there : there + n] = all_slots[k, 0:CONV, here : here + n]
            bias_ref[:, there : there + n] = all_slots[k, 4:5, here : here + n]
            gain_ref[:, there : there + n] = all_slots[k, 8:9, here : here + n]
        skip = dot(all_slots[k, 0:8, :WIDE], pick, AB, HIGH)
        both = jnp.concatenate([all_slots[k, 16:24, :128], skip])
        heads = heads + dot(both, head_map(k, block), AB, HIGH)
    dt_ref[...] = heads[0:1, :HEADS]
    log_ref[...] = heads[1:2, :HEADS]
    skip_ref[...] = heads[13:14, :HEADS]


def spread_small(sp, block, slots, d):
    one = shape((1, HEADS), F32)
    return call(
        "spread_small",
        functools.partial(spread_small_kernel, block),
        sp,
        slots,
        [
            shape((1, d), F32),
            shape((1, CONV, CONV_DIM), F32),
            shape((1, CONV_DIM), F32),
            one,
            one,
            one,
            shape((1, INNER), F32),
        ],
        12,
        scratch=[pltpu.VMEM((CTX, PACK, MIX), F32)],
    )


def sum_over_dp(x, dp, step, end):
    if dp & (dp - 1):
        return lax.psum(x, "dp") if step == 1 else x
    while step < end:
        x = x + lax.ppermute(x, "dp", [(i, i ^ step) for i in range(dp)])
        step *= 2
    return x


class Order:
    def __init__(self, sp):
        self.sp = sp

    def __call__(self, kernel, *args):
        out = kernel(self.sp, *args)
        self.after(out[0] if isinstance(out, (list, tuple)) else out)
        return out

    def after(self, x):
        self.sp, _ = lax.optimization_barrier((self.sp, x))

    def now(self, x):
        return lax.optimization_barrier((x, self.sp))[0]


def shards(
    tokens,
    cotangent,
    doc_lengths,
    norm_gain,
    w_in,
    conv_weight,
    conv_bias,
    dt_bias,
    a_log,
    d_skip,
    inner_gain,
    w_out,
):
    mine, place = lax.axis_index("section"), lax.axis_index("ctx")
    dp = lax.axis_size("dp")
    piece, d = tokens.shape[2], tokens.shape[3]
    seg_len = piece * CTX // SEGS
    direct = dp == 4 and w_out.shape[1] % HEAD == 0 and w_out.shape[1] * dp == WIDE
    block = w_out.shape[1] // HEAD if direct else LOCAL

    own_x = lax.dynamic_index_in_dim(tokens, mine, 0, False)[0]
    own_u = lax.dynamic_index_in_dim(cotangent, mine, 0, False)[0]
    lengths = lax.dynamic_index_in_dim(doc_lengths, mine, 0, False)[0]
    start = jnp.stack([place, mine, lax.axis_index("dp")]).astype(jnp.int32)
    sp = jnp.concatenate([start, jnp.cumsum(lengths) - lengths])
    run = Order(sp)
    if direct:
        carrier = Direct(run, mine, dp, block, w_in[0], w_out[0])
    else:
        carrier = Plain(mine, place, block, w_in[0], w_out[0])

    def natural(slots):
        return jnp.concatenate(slots).reshape(CTX, 2, piece // 2, d)

    rows_x = gather_slots(run, run.now(own_x))
    arrays = [norm_gain, conv_weight, conv_bias, dt_bias, a_log, d_skip, inner_gain]
    params = run(prepare, block, arrays)
    other = swap_core(params)
    params = [choose(mine == 0, params, other), choose(mine == 0, other, params)]
    carrier.prepare_gate()
    rows_x = natural(rows_x())
    conv0 = carrier.start_conv()
    run.after(rows_x)
    gate0 = carrier.start_gate(conv0)
    conv0 = carrier.trade_weights(conv0)
    rows_u = gather_slots(run, run.now(own_u))
    no_state, no_tail = jnp.zeros((STATE, WIDE), F32), jnp.zeros((16, MIX), BF16)

    def forward(layer, s, pieces, wc, state, tail, between=None):
        normed, conv_in, step_raw = run(project, pieces, params[layer], wc, seg_len)
        if between is not None:
            between()
        y, states, state, next_tail = run(
            scan_rows, s, conv_in, step_raw, params[layer], state, tail
        )
        return dict(
            normed=normed, conv_in=conv_in, step_raw=step_raw, y=y, states=states, tail=tail
        ), state, next_tail

    wc0 = run(carrier.conv_weights, conv0)
    conv1, gate1 = carrier.start_second()
    first, second = [None, None], [None, None]
    state, tail = no_state, no_tail
    first[0], state, tail = forward(0, 0, natural_slots(rows_x, 0), wc0, state, tail)
    first[1], state, tail = forward(0, 1, natural_slots(rows_x, 1), wc0, state, tail)
    rows_u = rows_u()
    gate0 = carrier.trade_weights(gate0)
    wg0, wo0 = run(carrier.gate_weights, gate0)
    stats, sums = [None, None], [None, None]
    for s in range(SEGS):
        saved = first[s]
        saved["gate"], stats[s], *sums[s] = run(
            out_rows, True, [], [], saved["normed"], saved["y"], params[0], wg0, wo0
        )
        if s == 0:
            sums[0] = scatter_start(*sums[0])

    def own_step(s):
        residual = natural_slots(rows_x, s)[:1]
        first[s]["stats"] = [stats[s]] + [tail_tile(x) for x in sums[s][1:4]]
        own, first[s]["branch"] = run(own_rows, False, first[s]["stats"], sums[s], residual)
        first[s]["own"] = own
        return gather_slots(run, own)

    sums[0] = scatter_slots(run, *sums[0])
    sums[1] = scatter_start(*[run.now(x) for x in sums[1]])
    middle = [own_step(0), None]
    sums[1] = scatter_slots(run, *sums[1])
    middle[0] = middle[0]()
    rows_u = natural(rows_u)
    run.after(rows_u)

    conv1 = carrier.trade_weights(conv1)
    wc1 = run(carrier.conv_weights, conv1)
    middle[1] = own_step(1)
    state, tail = no_state, no_tail
    parts, before = [], []

    def last_rows():
        middle[1] = middle[1]()

    for s in range(SEGS):
        between = last_rows if s == 0 else None
        second[s], state, tail = forward(1, s, middle[s], wc1, state, tail, between)
        if s == 0:
            run.after(middle[1][3:])
            gate1 = carrier.trade_weights(gate1)
    wg1, wo1 = run(carrier.gate_weights, gate1)
    for s in range(SEGS):
        saved = second[s]
        saved["gate"], stats, part = run(
            out_rows,
            False,
            before,
            natural_slots(rows_u, s),
            saved["normed"],
            saved["y"],
            params[1],
            wg1,
            wo1,
        )
        before = [stats]
        parts.append(part)
    stats = from_all(stats)
    part1 = run(collect, parts)
    hidden0 = run(natural_rows, middle)

    def gate_step(layer, s, saved, pieces, stats, first_stat, inners, wo):
        out = run(
            gate_back, pieces, stats, first_stat, inners, saved["y"], saved["gate"], params[layer], wo
        )
        saved.update(zip(("dy", "dgate", "gated", "u", "dgain"), out))

    def scan_step(layer, s, saved, dstate, later):
        saved["dconv"], saved["dcw"], saved["dhp"], dstate, later = run(
            scan_back,
            layer == 0,
            s,
            saved["conv_in"],
            saved["step_raw"],
            saved["dy"],
            saved["states"],
            saved["tail"],
            params[layer],
            dstate,
            later,
        )
        return dstate, later

    def of(saved, *names):
        return [[one[name] for one in saved] for name in names]

    def back_start(s):
        saved = second[s]
        return scatter_start(*run(input_back, True, saved["dconv"], saved["dgate"], wc1, wg1))

    def back_end(s, part):
        up, second[s]["dnorm"] = run(
            own_back,
            16,
            part,
            [far(first[s]["own"])],
            natural_slots(rows_u, s)[:1],
            params[1],
            far(first[s]["branch"]),
        )
        return gather_slots(run, up, 16)

    upper = [None, None]

    def lower_gate(s):
        inners = [head_tile(x) for x in upper[s][:4]]
        gate_step(0, s, first[s], upper[s], first[s]["stats"], 0, inners, wo0)

    for s in (1, 0):
        gate_step(1, s, second[s], natural_slots(rows_u, s), stats, 8 * s, [], wo1)
    gate1 = carrier.trade_grads(run(carrier.grad_gate, 1, *of(second, "normed", "dgate", "gated", "u")))
    part1 = scatter_start(*part1)
    dstate, later = no_state, jnp.zeros((8, MIX), F32)
    dstate, later = scan_step(1, 1, second[1], dstate, later)
    part1 = scatter_slots(run, *part1)
    gate1 = carrier.send(gate1)
    upper[1] = back_start(1)
    dstate, later = scan_step(1, 0, second[0], dstate, later)
    hidden1, _ = run(own_rows, True, stats, part1, [hidden0])
    upper[1] = scatter_slots(run, *upper[1])
    upper[0] = back_start(0)
    upper[1] = back_end(1, upper[1])
    conv1 = run(carrier.grad_conv, 1, *of(second, "normed", "dconv"))
    upper[1] = upper[1]()
    upper[0] = scatter_slots(run, *upper[0])
    conv1 = carrier.trade_grads([run.now(x) for x in conv1])
    lower_gate(1)
    conv1 = carrier.send(conv1)
    upper[0] = back_end(0, upper[0])
    dstate, later = no_state, jnp.zeros((8, MIX), F32)
    dstate, later = scan_step(0, 1, first[1], dstate, later)
    upper[0] = upper[0]()
    (part_1,) = run(input_back, False, first[1]["dconv"], first[1]["dgate"], wc0, wg0)
    lower_gate(0)
    gate0 = carrier.trade_grads(run(carrier.grad_gate, 0, *of(first, "normed", "dgate", "gated", "u")))
    grads1 = run(natural_rows, upper, 16)
    gate0 = carrier.send(gate0)
    dstate, later = scan_step(0, 0, first[0], dstate, later)
    conv0 = carrier.trade_grads(run(carrier.grad_conv, 0, *of(first, "normed", "dconv")))
    (part_0,) = run(input_back, False, first[0]["dconv"], first[0]["dgate"], wc0, wg0)
    conv0 = carrier.send(conv0)
    part = scatter_start(*run(collect, [far(part_0), far(part_1)]))
    part = scatter_slots(run, *part)
    carrier.early(conv1, gate1, gate0)
    branch = jnp.zeros((piece, d), F32)
    grads0, dnorm0 = run(own_back, 0, part, [own_x], [grads1], params[0], branch)
    carrier.early_trade()
    small = [
        of(first, "dcw", "dhp", "dgain") + [[dnorm0]],
        of(second, "dcw", "dhp", "dgain", "dnorm"),
    ]
    keep, small_sent = run(gather_small, small)
    total = sum_over_dp(keep + swap_core(small_sent), dp, 1, dp)
    carrier.late(conv0)
    carrier.late_trade()
    total = from_all(run.now(total))
    shard_in, shard_out = carrier.gradients()
    norm, taps, bias, dt, log, skip, gain = run(spread_small, block, total, d)

    def to_layers(a, b):
        here, there = choose(mine == 0, a, b), swap_core(choose(mine == 0, b, a))
        both = jnp.stack([choose(mine == 0, here, there), choose(mine == 0, there, here)])
        return both[None, :, None]

    return (
        to_layers(hidden0, hidden1),
        to_layers(grads0, grads1),
        norm,
        shard_in[None],
        taps,
        bias,
        dt,
        log,
        skip,
        gain,
        shard_out[None],
    )


def solution(mesh):
    in_specs = (
        P(None, "dp", "ctx", None),
        P(None, "dp", "ctx", None),
        P(None, "dp", None),
        P("section", None),
        P("section", ("dp", "ctx"), None),
        P("section", None, None),
        P("section", None),
        P("section", None),
        P("section", None),
        P("section", None),
        P("section", None),
        P("section", ("dp", "ctx"), None),
    )
    out_specs = (
        P("section", None, "dp", "ctx", None),
        P("section", None, "dp", "ctx", None),
        P("section", None),
        P("section", ("dp", "ctx"), None),
        P("section", None, None),
        P("section", None),
        P("section", None),
        P("section", None),
        P("section", None),
        P("section", None),
        P("section", ("dp", "ctx"), None),
    )
    return jax.shard_map(shards, mesh=mesh, in_specs=in_specs, out_specs=out_specs, check_vma=False)
```

profile of v0, /device:TPU:0, one launch (start us, length us, event | category | flops | bytes accessed | tf_op | source)
XLA Modules:
  0.0 553.5 jit_solution(13332742366203306844)
XLA Ops:
  16.3 5.3 collective-permute-done.refs_1_
  21.6 5.9 %collective-permute-done.1.refs_2_ = bf16[96,1280]{1,0:T(8,128)(2,1)S(1)} collective-permute-done((bf16[96,1280]{1,0:T(8,128)(2,1)S(1)}, bf16[96,1280]{1,0:T(8,128)(2,1)S(1)}, u32[]{:S(2)}, u32[]{:S(2)}) %collective-permute-start.1) | collective-permute-done | bytes 245792 | tf_op jit(solution)/shard_map/ppermute | solution.py:48
  39.0 16.9 %collective-permute-done.5.refs_3_ = bf16[96,768]{1,0:T(8,128)(2,1)S(1)} collective-permute-done((bf16[96,768]{1,0:T(8,128)(2,1)}, bf16[96,768]{1,0:T(8,128)(2,1)S(1)}, u32[]{:S(2)}, u32[]{:S(2)}) %collective-permute-start.5) | collective-permute-done | bytes 147488 | tf_op jit(solution)/shard_map/ppermute | solution.py:48
  64.1 7.2 %collective-permute-done.8 = bf16[128,1536]{1,0:T(8,128)(2,1)S(1)} collective-permute-done((bf16[128,1536]{1,0:T(8,128)(2,1)S(1)}, bf16[128,1536]{1,0:T(8,128)(2,1)S(1)}, u32[]{:S(2)}, u32[]{:S(2)}) %collective-permute-start.8) | collective-permute-done | bytes 393248 | tf_op jit(solution)/shard_map/ppermute | solution.py:48
  85.5 5.1 project.4
  90.7 7.6 %scan_rows.4 = (f32[512,768]{1,0:T(8,128)S(1)}, f32[512,768]{1,0:T(8,128)}, f32[128,768]{1,0:T(8,128)S(1)}, bf16[16,1024]{1,0:T(8,128)(2,1)S(1)}) custom-call(s32[7]{0:T(128)S(1)} %pad_add_fusion.sp, bf16[512,1024]{1,0:T(8,128)(2,1)S(1)} %get-tuple-element.310.ci_ref.prev_ref, f32[512,128]{1,0:T(8,128)S(1)} %get-tuple-element.311.raw_ref, ...), custom_call_target="tpu_custom_call" | custom-call | flops 8000000000 | bytes 1 | tf_op jit(solution)/shard_map/scan_rows/pallas_call | solution.py:114
  99.5 4.4 project.5
  104.0 7.8 %scan_rows.5 = (f32[512,768]{1,0:T(8,128)S(1)}, f32[512,768]{1,0:T(8,128)}, f32[128,768]{1,0:T(8,128)}, bf16[16,1024]{1,0:T(8,128)(2,1)}) custom-call(s32[7]{0:T(128)S(1)} %pad_add_fusion.sp, bf16[512,1024]{1,0:T(8,128)(2,1)S(1)} %get-tuple-element.316.ci_ref.prev_ref, f32[512,128]{1,0:T(8,128)S(1)} %get-tuple-element.317.raw_ref, ...), custom_call_target="tpu_custom_call" | custom-call | flops 8000000000 | bytes 1 | tf_op jit(solution)/shard_map/scan_rows/pallas_call | solution.py:114
  113.8 12.8 %all-gather.11.cloned.1.call-done = bf16[16,96,768]{2,1,0:T(8,128)(2,1)} async-done(((bf16[4,96,768]{2,1,0:T(8,128)(2,1)}), bf16[16,96,768]{2,1,0:T(8,128)(2,1)}) %all-gather.11.cloned.1.call-update) | async-done | bytes 2359312 | tf_op jit(solution)/shard_map/all_gather | solution.py:1221
  146.7 4.5 out_rows.5
  159.4 6.9 %collective-permute-done.20.refs_8_ = bf16[64,1536]{1,0:T(8,128)(2,1)S(1)} collective-permute-done((bf16[64,1536]{1,0:T(8,128)(2,1)S(1)}, bf16[64,1536]{1,0:T(8,128)(2,1)S(1)}, u32[]{:S(2)}, u32[]{:S(2)}) %collective-permute-start.20) | collective-permute-done | bytes 196640 | tf_op jit(solution)/shard_map/ppermute | solution.py:48
  202.6 4.4 collective-permute-done.32.refs_1_.refs_6_
  210.4 7.7 %scan_rows.6 = (f32[512,768]{1,0:T(8,128)S(1)}, f32[512,768]{1,0:T(8,128)}, f32[128,768]{1,0:T(8,128)S(1)}, bf16[16,1024]{1,0:T(8,128)(2,1)S(1)}) custom-call(s32[7]{0:T(128)S(1)} %pad_add_fusion.sp, bf16[512,1024]{1,0:T(8,128)(2,1)S(1)} %get-tuple-element.374.ci_ref.prev_ref, f32[512,128]{1,0:T(8,128)S(1)} %get-tuple-element.375.raw_ref, ...), custom_call_target="tpu_custom_call" | custom-call | flops 8000000000 | bytes 1 | tf_op jit(solution)/shard_map/scan_rows/pallas_call | solution.py:114
  226.6 7.8 %scan_rows.7 = (f32[512,768]{1,0:T(8,128)S(1)}, f32[512,768]{1,0:T(8,128)}, f32[128,768]{1,0:T(8,128)}, bf16[16,1024]{1,0:T(8,128)(2,1)}) custom-call(s32[7]{0:T(128)S(1)} %pad_add_fusion.sp, bf16[512,1024]{1,0:T(8,128)(2,1)S(1)} %get-tuple-element.383.ci_ref.prev_ref, f32[512,128]{1,0:T(8,128)S(1)} %get-tuple-element.384.raw_ref, ...), custom_call_target="tpu_custom_call" | custom-call | flops 8000000000 | bytes 1 | tf_op jit(solution)/shard_map/scan_rows/pallas_call | solution.py:114
  236.3 5.7 %out_rows.6 = (f32[512,768]{1,0:T(8,128)S(1)}, f32[8,512]{1,0:T(8,128)S(1)}, bf16[512,1536]{1,0:T(8,128)(2,1)S(1)}) custom-call(s32[7]{0:T(128)S(1)} %pad_add_fusion.sp, bf16[4,2,128,1536]{3,2,1,0:T(8,128)(2,1)} %bitcast.13.refs_0_.refs_1_.refs_2_.refs_3_.refs_4_.refs_6_, bf16[4,2,128,1536]{3,2,1,0:T(8,128)(2,1)} %bitcast.13.refs_0_.refs_1_.refs_2_.refs_3_.refs_4_.refs_6_, ...), custom_call_target="tpu_custom_call" | custom-call | flops 4000000000 | bytes 1 | tf_op jit(solution)/shard_map/out_rows/pallas_call | solution.py:114
  242.0 5.7 %out_rows.7 = (f32[512,768]{1,0:T(8,128)S(1)}, f32[16,512]{1,0:T(8,128)S(1)}, bf16[512,1536]{1,0:T(8,128)(2,1)S(1)}) custom-call(s32[7]{0:T(128)S(1)} %pad_add_fusion.sp, f32[8,512]{1,0:T(8,128)S(1)} %get-tuple-element.396.refs_0_, bf16[4,2,128,1536]{3,2,1,0:T(8,128)(2,1)} %bitcast.13.refs_0_.refs_1_.refs_2_.refs_3_.refs_4_.refs_6_, ...), custom_call_target="tpu_custom_call" | custom-call | flops 4000000000 | bytes 1 | tf_op jit(solution)/shard_map/out_rows/pallas_call | solution.py:114
  259.7 4.1 gate_back.5
  263.9 8.5 %grad_gate.2 = (bf16[4,4,96,768]{3,2,1,0:T(8,128)(2,1)S(1)}, bf16[4,4,96,768]{3,2,1,0:T(8,128)(2,1)S(1)}) custom-call(s32[7]{0:T(128)S(1)} %pad_add_fusion.sp, bf16[512,1536]{1,0:T(8,128)(2,1)S(1)} %copy-done.36, bf16[512,1536]{1,0:T(8,128)(2,1)S(1)} %get-tuple-element.381.refs_5_.refs_1_.n1_ref, bf16[512,768]{1,0:T(8,128)(2,1)S(1)} %get-tuple-element.409.refs_2_.dg_ref, ...), custom_call_target="tpu_custom_call" | custom-call | flops 8000000000 | bytes 1 | tf_op jit(solution)/shard_map/grad_gate/pallas_call | solution.py:114
  273.7 15.7 %scan_back.4 = (bf16[512,1152]{1,0:T(8,128)(2,1)S(1)}, f32[8,1024]{1,0:T(8,128)S(1)}, f32[8,128]{1,0:T(8,128)S(1)}, f32[128,768]{1,0:T(8,128)S(1)}, f32[8,1024]{1,0:T(8,128)S(1)}) custom-call(s32[7]{0:T(128)S(1)} %pad_add_fusion.sp, bf16[512,1024]{1,0:T(8,128)(2,1)S(1)} %get-tuple-element.383.ci_ref.prev_ref, ...), custom_call_target="tpu_custom_call" | custom-call | flops 16000000000 | bytes 1 | tf_op jit(solution)/shard_map/scan_back/pallas_call | solution.py:114
  309.6 16.6 %scan_back.5 = (bf16[512,1152]{1,0:T(8,128)(2,1)S(1)}, f32[8,1024]{1,0:T(8,128)S(1)}, f32[8,128]{1,0:T(8,128)S(1)}, f32[128,768]{1,0:T(8,128)}, f32[8,1024]{1,0:T(8,128)}) custom-call(s32[7]{0:T(128)S(1)} %pad_add_fusion.sp, bf16[512,1024]{1,0:T(8,128)(2,1)S(1)} %copy-done.189, bf16[512,1024]{1,0:T(8,128)(2,1)S(1)} %copy-done.189, ...), custom_call_target="tpu_custom_call" | custom-call | flops 16000000000 | bytes 1 | tf_op jit(solution)/shard_map/scan_back/pallas_call | solution.py:114
  344.8 5.9 %grad_conv.2 = (bf16[4,4,96,640]{3,2,1,0:T(8,128)(2,1)S(1)}, bf16[4,4,96,640]{3,2,1,0:T(8,128)(2,1)S(1)}) custom-call(s32[7]{0:T(128)S(1)} %pad_add_fusion.sp, bf16[512,1536]{1,0:T(8,128)(2,1)S(1)} %copy-done.37, bf16[512,1536]{1,0:T(8,128)(2,1)S(1)} %copy-done.39, bf16[512,1152]{1,0:T(8,128)(2,1)S(1)} %get-tuple-element.433.dc_ref.d0_ref, ...), custom_call_target="tpu_custom_call" | custom-call | flops 6000000000 | bytes 1 | tf_op jit(solution)/shard_map/grad_conv/pallas_call | solution.py:114
  350.7 4.8 collective-permute-done.50.refs_1_.refs_10_.refs_6_
  361.6 4.4 collective-permute-done.55.refs_4_.refs_9_
  382.0 17.5 %scan_back.6 = (bf16[512,1152]{1,0:T(8,128)(2,1)S(1)}, f32[8,1024]{1,0:T(8,128)S(1)}, f32[8,128]{1,0:T(8,128)S(1)}, f32[128,768]{1,0:T(8,128)S(1)}, f32[8,1024]{1,0:T(8,128)S(1)}) custom-call(s32[7]{0:T(128)S(1)} %pad_add_fusion.sp, bf16[512,1024]{1,0:T(8,128)(2,1)} %copy-done.132, bf16[512,1024]{1,0:T(8,128)(2,1)} %copy-done.132, f32[512,128]{1,0:T(8,128)} %copy-done.144, ...), custom_call_target="tpu_custom_call" | custom-call | flops 16000000000 | bytes 1 | tf_op jit(solution)/shard_map/scan_back/pallas_call | solution.py:114
  411.1 4.3 gate_back.7
  415.6 8.1 %grad_gate.3 = (bf16[4,4,96,768]{3,2,1,0:T(8,128)(2,1)S(1)}, bf16[4,4,96,768]{3,2,1,0:T(8,128)(2,1)S(1)}) custom-call(s32[7]{0:T(128)S(1)} %pad_add_fusion.sp, bf16[512,1536]{1,0:T(8,128)(2,1)S(1)} %copy-done.124, bf16[512,1536]{1,0:T(8,128)(2,1)S(1)} %copy-done.128, bf16[512,768]{1,0:T(8,128)(2,1)S(1)} %get-tuple-element.481.refs_2_.dg_ref, ...), custom_call_target="tpu_custom_call" | custom-call | flops 8000000000 | bytes 1 | tf_op jit(solution)/shard_map/grad_gate/pallas_call | solution.py:114
  431.0 18.7 %scan_back.7 = (bf16[512,1152]{1,0:T(8,128)(2,1)S(1)}, f32[8,1024]{1,0:T(8,128)S(1)}, f32[8,128]{1,0:T(8,128)S(1)}, f32[128,768]{1,0:T(8,128)}, f32[8,1024]{1,0:T(8,128)}) custom-call(s32[7]{0:T(128)S(1)} %pad_add_fusion.sp, bf16[512,1024]{1,0:T(8,128)(2,1)} %copy-done.131, bf16[512,1024]{1,0:T(8,128)(2,1)} %copy-done.131, f32[512,128]{1,0:T(8,128)} %copy-done.143, ...), custom_call_target="tpu_custom_call" | custom-call | flops 16000000000 | bytes 1 | tf_op jit(solution)/shard_map/scan_back/pallas_call | solution.py:114
  449.8 5.9 %grad_conv.3 = (bf16[4,4,96,640]{3,2,1,0:T(8,128)(2,1)S(1)}, bf16[4,4,96,640]{3,2,1,0:T(8,128)(2,1)S(1)}) custom-call(s32[7]{0:T(128)S(1)} %pad_add_fusion.sp, bf16[512,1536]{1,0:T(8,128)(2,1)S(1)} %copy-done.125, bf16[512,1536]{1,0:T(8,128)(2,1)S(1)} %copy-done.129, bf16[512,1152]{1,0:T(8,128)(2,1)S(1)} %get-tuple-element.494.d0_ref.dc_ref, ...), custom_call_target="tpu_custom_call" | custom-call | flops 6000000000 | bytes 1 | tf_op jit(solution)/shard_map/grad_conv/pallas_call | solution.py:114
  469.6 17.6 %collective-permute-done.65.from_x_ref.refs_1_ = bf16[256,1536]{1,0:T(8,128)(2,1)S(1)} collective-permute-done((bf16[256,1536]{1,0:T(8,128)(2,1)S(1)}, bf16[256,1536]{1,0:T(8,128)(2,1)S(1)}, u32[]{:S(2)}, u32[]{:S(2)}) %collective-permute-start.65) | collective-permute-done | bytes 786464 | tf_op jit(solution)/shard_map/ppermute | solution.py:48
  498.4 4.3 collective-permute-done.67.refs_3_
  508.8 4.1 collective-permute-done.72.refs_3_
  517.3 4.1 collective-permute-done.79
  (721 shorter events, 275.9 us)
Async XLA Ops:
  7.2 68.0 %all-gather.9.cloned.1.call-start = ((), (), s32[]{:S(2)}) async-start(), calls=%async_computation.8 | async-start | bytes 2457600 | tf_op jit(solution)/shard_map/all_gather | solution.py:1221
  31.1 95.5 %all-gather.11.cloned.1.call-start = ((), (), s32[]{:S(2)}) async-start(), calls=%async_computation.9 | async-start | bytes 2949120 | tf_op jit(solution)/shard_map/all_gather | solution.py:1221
  31.3 28.4 %collective-permute-start.6 = (bf16[256,1536]{1,0:T(8,128)(2,1)S(1)}, bf16[256,1536]{1,0:T(8,128)(2,1)S(1)}, u32[]{:S(2)}, u32[]{:S(2)}) collective-permute-start(bf16[256,1536]{1,0:T(8,128)(2,1)S(1)} %dynamic-slice_bitcast_fusion.1.refs_5_), channel_id=1, source_target_pairs={{0,1},{1,0},{2,3},{3,2},{4,5},{5,4},{6,7},{7,6},{8,9},{9,8},{10,11... | collective-permute-start | bytes 2359304 | tf_op jit(solution)/shard_map/ppermute | solution.py:48
  32.6 27.1 %collective-permute-start.7 = (bf16[256,1536]{1,0:T(8,128)(2,1)S(1)}, bf16[256,1536]{1,0:T(8,128)(2,1)S(1)}, u32[]{:S(2)}, u32[]{:S(2)}) collective-permute-start(bf16[256,1536]{1,0:T(8,128)(2,1)S(1)} %dynamic-slice_bitcast_fusion.1.refs_5_), channel_id=1, source_target_pairs={{0,2},{1,3},{2,0},{3,1},{4,6},{5,7},{6,4},{7,5},{8,10},{9,11},{10,... | collective-permute-start | bytes 2359304 | tf_op jit(solution)/shard_map/ppermute | solution.py:48
  33.4 22.5 %collective-permute-start.5 = (bf16[96,768]{1,0:T(8,128)(2,1)}, bf16[96,768]{1,0:T(8,128)(2,1)S(1)}, u32[]{:S(2)}, u32[]{:S(2)}) collective-permute-start(bf16[96,768]{1,0:T(8,128)(2,1)} %get-tuple-element.297), channel_id=1, source_target_pairs={{0,3},{1,2},{2,1},{3,0},{4,7},{5,6},{6,5},{7,4},{8,11},{9,10},{10,... | collective-permute-start | bytes 442376 | tf_op jit(solution)/shard_map/ppermute | solution.py:48
  34.8 23.4 %collective-permute-start.4 = (bf16[96,768]{1,0:T(8,128)(2,1)}, bf16[96,768]{1,0:T(8,128)(2,1)S(1)}, u32[]{:S(2)}, u32[]{:S(2)}) collective-permute-start(bf16[96,768]{1,0:T(8,128)(2,1)} %get-tuple-element.295), channel_id=1, source_target_pairs={{0,2},{1,3},{2,0},{3,1},{4,6},{5,7},{6,4},{7,5},{8,10},{9,11},{10,... | collective-permute-start | bytes 442376 | tf_op jit(solution)/shard_map/ppermute | solution.py:48
  36.4 21.8 %collective-permute-start.3 = (bf16[96,768]{1,0:T(8,128)(2,1)S(1)}, bf16[96,768]{1,0:T(8,128)(2,1)S(1)}, u32[]{:S(2)}, u32[]{:S(2)}) collective-permute-start(bf16[96,768]{1,0:T(8,128)(2,1)S(1)} %get-tuple-element.293), channel_id=1, source_target_pairs={{0,1},{1,0},{2,3},{3,2},{4,5},{5,4},{6,7},{7,6},{8,9},{9,8},{10,11... | collective-permute-start | bytes 442376 | tf_op jit(solution)/shard_map/ppermute | solution.py:48
  76.3 108.6 %all-gather.13.cloned.1.call-start = ((), (), s32[]{:S(2)}) async-start(), calls=%async_computation.10 | async-start | bytes 2457600 | tf_op jit(solution)/shard_map/all_gather | solution.py:1221
  79.3 33.6 %collective-permute-start.13 = (bf16[256,1536]{1,0:T(8,128)(2,1)S(1)}, bf16[256,1536]{1,0:T(8,128)(2,1)S(1)}, u32[]{:S(2)}, u32[]{:S(2)}) collective-permute-start(bf16[256,1536]{1,0:T(8,128)(2,1)S(1)} %dynamic-slice_bitcast_fusion), channel_id=1, source_target_pairs={{0,1},{1,0},{2,3},{3,2},{4,5},{5,4},{6,7},{7,6},{8,9},{9,8},{10,11... | collective-permute-start | bytes 2359304 | tf_op jit(solution)/shard_map/ppermute | solution.py:48
  80.9 33.0 %collective-permute-start.14 = (bf16[256,1536]{1,0:T(8,128)(2,1)S(1)}, bf16[256,1536]{1,0:T(8,128)(2,1)}, u32[]{:S(2)}, u32[]{:S(2)}) collective-permute-start(bf16[256,1536]{1,0:T(8,128)(2,1)S(1)} %dynamic-slice_bitcast_fusion), channel_id=1, source_target_pairs={{0,2},{1,3},{2,0},{3,1},{4,6},{5,7},{6,4},{7,5},{8,10},{9,11},{10,... | collective-permute-start | bytes 2359304 | tf_op jit(solution)/shard_map/ppermute | solution.py:48
  126.7 94.7 %all-gather.15.cloned.1.call-start = ((), (), s32[]{:S(2)}) async-start(), calls=%async_computation.11 | async-start | bytes 2949120 | tf_op jit(solution)/shard_map/all_gather | solution.py:1221
  145.6 25.8 %collective-permute-start.25 = (bf16[128,1536]{1,0:T(8,128)(2,1)}, bf16[128,1536]{1,0:T(8,128)(2,1)}, u32[]{:S(2)}, u32[]{:S(2)}) collective-permute-start(bf16[128,1536]{1,0:T(8,128)(2,1)} %slice.50), channel_id=1, source_target_pairs={{0,1},{1,0},{2,3},{3,2},{4,5},{5,4},{6,7},{7,6},{8,9},{9,8},{10,11... | collective-permute-start | bytes 1179656 | tf_op jit(solution)/shard_map/ppermute | solution.py:48
  146.1 28.5 %collective-permute-start.26 = (bf16[128,1536]{1,0:T(8,128)(2,1)}, bf16[128,1536]{1,0:T(8,128)(2,1)}, u32[]{:S(2)}, u32[]{:S(2)}) collective-permute-start(bf16[128,1536]{1,0:T(8,128)(2,1)} %slice.51), channel_id=1, source_target_pairs={{0,2},{1,3},{2,0},{3,1},{4,6},{5,7},{6,4},{7,5},{8,10},{9,11},{10,... | collective-permute-start | bytes 1179656 | tf_op jit(solution)/shard_map/ppermute | solution.py:48
  158.5 334.1 %reduce-scatter.7.cloned.1.call-start = ((), (), s32[]{:S(2)}) async-start(), calls=%async_computation.5 | async-start | bytes 2949120 | tf_op jit(solution)/shard_map/reduce_scatter | solution.py:1254
  158.7 17.7 %collective-permute-start.22 = (bf16[144,1536]{1,0:T(8,128)(2,1)}, bf16[144,1536]{1,0:T(8,128)(2,1)S(1)}, u32[]{:S(2)}, u32[]{:S(2)}) collective-permute-start(bf16[144,1536]{1,0:T(8,128)(2,1)} %get-tuple-element.349), channel_id=1, source_target_pairs={{0,2},{1,3},{2,0},{3,1},{4,6},{5,7},{6,4},{7,5},{8,10},{9,11},{10,... | collective-permute-start | bytes 1327112 | tf_op jit(solution)/shard_map/ppermute | solution.py:48
  272.4 23.9 %collective-permute-start.42 = (bf16[4,4,96,768]{3,2,1,0:T(8,128)(2,1)S(1)}, bf16[4,4,96,768]{3,2,1,0:T(8,128)(2,1)S(1)}, u32[]{:S(2)}, u32[]{:S(2)}) collective-permute-start(bf16[4,4,96,768]{3,2,1,0:T(8,128)(2,1)S(1)} %get-tuple-element.426), channel_id=1, source_target_pairs={{0,16},{16,0},{1,17},{17,1},{2,18},{18,2},{3,19},{19,3},{4,20},{20... | collective-permute-start | bytes 7077896 | tf_op jit(solution)/shard_map/ppermute | solution.py:44
  272.5 20.0 %collective-permute-start.40 = (bf16[256,1536]{1,0:T(8,128)(2,1)S(1)}, bf16[256,1536]{1,0:T(8,128)(2,1)S(1)}, u32[]{:S(2)}, u32[]{:S(2)}) collective-permute-start(bf16[256,1536]{1,0:T(8,128)(2,1)S(1)} %get-tuple-element.420), channel_id=1, source_target_pairs={{0,1},{1,0},{2,3},{3,2},{4,5},{5,4},{6,7},{7,6},{8,9},{9,8},{10,11... | collective-permute-start | bytes 2359304 | tf_op jit(solution)/shard_map/ppermute | solution.py:48
  273.1 19.6 %collective-permute-start.41 = (bf16[256,1536]{1,0:T(8,128)(2,1)S(1)}, bf16[256,1536]{1,0:T(8,128)(2,1)S(1)}, u32[]{:S(2)}, u32[]{:S(2)}) collective-permute-start(bf16[256,1536]{1,0:T(8,128)(2,1)S(1)} %get-tuple-element.421), channel_id=1, source_target_pairs={{0,2},{1,3},{2,0},{3,1},{4,6},{5,7},{6,4},{7,5},{8,10},{9,11},{10,... | collective-permute-start | bytes 2359304 | tf_op jit(solution)/shard_map/ppermute | solution.py:48
  294.3 31.9 %collective-permute-start.43 = (bf16[128,1536]{1,0:T(8,128)(2,1)}, bf16[128,1536]{1,0:T(8,128)(2,1)}, u32[]{:S(2)}, u32[]{:S(2)}) collective-permute-start(bf16[128,1536]{1,0:T(8,128)(2,1)} %get-tuple-element.424), channel_id=1, source_target_pairs={{0,1},{1,0},{2,3},{3,2},{4,5},{5,4},{6,7},{7,6},{8,9},{9,8},{10,11... | collective-permute-start | bytes 1179656 | tf_op jit(solution)/shard_map/ppermute | solution.py:48
  295.7 30.4 %collective-permute-start.44 = (bf16[128,1536]{1,0:T(8,128)(2,1)}, bf16[128,1536]{1,0:T(8,128)(2,1)}, u32[]{:S(2)}, u32[]{:S(2)}) collective-permute-start(bf16[128,1536]{1,0:T(8,128)(2,1)} %get-tuple-element.435), channel_id=1, source_target_pairs={{0,2},{1,3},{2,0},{3,1},{4,6},{5,7},{6,4},{7,5},{8,10},{9,11},{10,... | collective-permute-start | bytes 1179656 | tf_op jit(solution)/shard_map/ppermute | solution.py:48
  298.9 193.7 %reduce-scatter.5.cloned.1.call-start = ((), (), s32[]{:S(2)}) async-start(), calls=%async_computation.4 | async-start | bytes 2457600 | tf_op jit(solution)/shard_map/reduce_scatter | solution.py:1254
  307.7 22.9 %collective-permute-start.46 = (bf16[128,1536]{1,0:T(8,128)(2,1)S(1)}, bf16[128,1536]{1,0:T(8,128)(2,1)S(1)}, u32[]{:S(2)}, u32[]{:S(2)}) collective-permute-start(bf16[128,1536]{1,0:T(8,128)(2,1)S(1)} %get-tuple-element.438), channel_id=1, source_target_pairs={{0,1},{1,0},{2,3},{3,2},{4,5},{5,4},{6,7},{7,6},{8,9},{9,8},{10,11... | collective-permute-start | bytes 1179656 | tf_op jit(solution)/shard_map/ppermute | solution.py:48
  308.0 22.5 %collective-permute-start.47 = (bf16[128,1536]{1,0:T(8,128)(2,1)S(1)}, bf16[128,1536]{1,0:T(8,128)(2,1)S(1)}, u32[]{:S(2)}, u32[]{:S(2)}) collective-permute-start(bf16[128,1536]{1,0:T(8,128)(2,1)S(1)} %get-tuple-element.439), channel_id=1, source_target_pairs={{0,2},{1,3},{2,0},{3,1},{4,6},{5,7},{6,4},{7,5},{8,10},{9,11},{10,... | collective-permute-start | bytes 1179656 | tf_op jit(solution)/shard_map/ppermute | solution.py:48
  337.6 19.0 %collective-permute-start.52 = (bf16[128,1536]{1,0:T(8,128)(2,1)S(1)}, bf16[128,1536]{1,0:T(8,128)(2,1)S(1)}, u32[]{:S(2)}, u32[]{:S(2)}) collective-permute-start(bf16[128,1536]{1,0:T(8,128)(2,1)S(1)} %get-tuple-element.453), channel_id=1, source_target_pairs={{0,1},{1,0},{2,3},{3,2},{4,5},{5,4},{6,7},{7,6},{8,9},{9,8},{10,11... | collective-permute-start | bytes 1179656 | tf_op jit(solution)/shard_map/ppermute | solution.py:48
  338.2 18.4 %collective-permute-start.53 = (bf16[128,1536]{1,0:T(8,128)(2,1)S(1)}, bf16[128,1536]{1,0:T(8,128)(2,1)S(1)}, u32[]{:S(2)}, u32[]{:S(2)}) collective-permute-start(bf16[128,1536]{1,0:T(8,128)(2,1)S(1)} %get-tuple-element.454), channel_id=1, source_target_pairs={{0,2},{1,3},{2,0},{3,1},{4,6},{5,7},{6,4},{7,5},{8,10},{9,11},{10,... | collective-permute-start | bytes 1179656 | tf_op jit(solution)/shard_map/ppermute | solution.py:48
  379.8 21.8 %collective-permute-start.59 = (bf16[144,1536]{1,0:T(8,128)(2,1)}, bf16[144,1536]{1,0:T(8,128)(2,1)}, u32[]{:S(2)}, u32[]{:S(2)}) collective-permute-start(bf16[144,1536]{1,0:T(8,128)(2,1)} %get-tuple-element.469.refs_0_.refs_9_), channel_id=1, source_target_pairs={{0,1},{1,0},{2,3},{3,2},{4,5},{5,4},{6,7},{7,6},{8,9},{9,8},{10,11... | collective-permute-start | bytes 1327112 | tf_op jit(solution)/shard_map/ppermute | solution.py:48
  380.9 20.7 %collective-permute-start.60 = (bf16[144,1536]{1,0:T(8,128)(2,1)}, bf16[144,1536]{1,0:T(8,128)(2,1)}, u32[]{:S(2)}, u32[]{:S(2)}) collective-permute-start(bf16[144,1536]{1,0:T(8,128)(2,1)} %get-tuple-element.469.refs_0_.refs_9_), channel_id=1, source_target_pairs={{0,2},{1,3},{2,0},{3,1},{4,6},{5,7},{6,4},{7,5},{8,10},{9,11},{10,... | collective-permute-start | bytes 1327112 | tf_op jit(solution)/shard_map/ppermute | solution.py:48
  382.0 110.6 %reduce-scatter.9.cloned.1.call-start = ((), (), s32[]{:S(2)}) async-start(), calls=%async_computation.6 | async-start | bytes 2949120 | tf_op jit(solution)/shard_map/reduce_scatter | solution.py:1254
  430.9 92.3 %reduce-scatter.11.cloned.1.call-start = ((), (), s32[]{:S(2)}) async-start(), calls=%async_computation.7 | async-start | bytes 2457600 | tf_op jit(solution)/shard_map/reduce_scatter | solution.py:1254
  467.4 19.8 %collective-permute-start.65 = (bf16[256,1536]{1,0:T(8,128)(2,1)S(1)}, bf16[256,1536]{1,0:T(8,128)(2,1)S(1)}, u32[]{:S(2)}, u32[]{:S(2)}) collective-permute-start(bf16[256,1536]{1,0:T(8,128)(2,1)S(1)} %get-tuple-element.503), channel_id=1, source_target_pairs={{0,1},{1,0},{2,3},{3,2},{4,5},{5,4},{6,7},{7,6},{8,9},{9,8},{10,11... | collective-permute-start | bytes 2359304 | tf_op jit(solution)/shard_map/ppermute | solution.py:48
  468.5 19.5 %collective-permute-start.66 = (bf16[256,1536]{1,0:T(8,128)(2,1)S(1)}, bf16[256,1536]{1,0:T(8,128)(2,1)S(1)}, u32[]{:S(2)}, u32[]{:S(2)}) collective-permute-start(bf16[256,1536]{1,0:T(8,128)(2,1)S(1)} %get-tuple-element.504), channel_id=1, source_target_pairs={{0,2},{1,3},{2,0},{3,1},{4,6},{5,7},{6,4},{7,5},{8,10},{9,11},{10,... | collective-permute-start | bytes 2359304 | tf_op jit(solution)/shard_map/ppermute | solution.py:48
  515.4 19.3 %collective-permute-start.69 = (bf16[256,1536]{1,0:T(8,128)(2,1)}, bf16[256,1536]{1,0:T(8,128)(2,1)}, u32[]{:S(2)}, u32[]{:S(2)}) collective-permute-start(bf16[256,1536]{1,0:T(8,128)(2,1)} %broadcast_select_fusion), channel_id=1, source_target_pairs={{0,16},{16,0},{1,17},{17,1},{2,18},{18,2},{3,19},{19,3},{4,20},{20... | collective-permute-start | bytes 2359304 | tf_op jit(solution)/shard_map/ppermute | solution.py:44
  (287 other events, 2678.2 us)
Sparse Core Ops, SparseCore 0:
  31.3 43.8 all-gather.8
  77.3 49.3 all-gather.10
  128.3 42.3 all-gather.12
  172.1 49.3 all-gather.14
  299.0 45.9 reduce-scatter.6
  382.1 39.2 reduce-scatter.4
  431.1 46.0 reduce-scatter.8
  479.5 40.9 reduce-scatter.10
where the time goes:
time: 558 us; the launch traced here: 553 us
  Pallas kernels  252 us (45%)
  waiting for transfers between devices  138 us (25%)
  starting transfers between devices  79.7 us (14%)
  local copies, waits for them, and re-layouts  56.1 us (10%)
  between operations  17.2 us (3%)
  other arithmetic  10.2 us (2%)
    pallas_call x63, Pallas kernels, call(): pl.pallas_call(kernel, grid_spec=pltpu.PrefetchScalarGridSpec(num_scalar_...  252 us
    ppermute x66, waiting for transfers between devices, flip(): return lax.ppermute(x, 'ctx', [(i, i ^ bits) for i in range(CTX)])  109 us
    ppermute x66, starting transfers between devices, flip(): return lax.ppermute(x, 'ctx', [(i, i ^ bits) for i in range(CTX)])  74.5 us
    unnamed x462, local copies, waits for them, and re-layouts  46.5 us
    all_gather x4, waiting for transfers between devices, gathered(): return lax.all_gather(x, 'dp', axis=0)  17.4 us
  transfers between devices with their start and end apart: 92, of which 39 were waited for; matrix products, arithmetic and copies ran while one was open for 5% of the time, Pallas kernels for 39%

commit v1 on v0

--- a/solution.py
+++ b/solution.py
@@ -1719,16 +1719,16 @@
     dstate, later = no_state, jnp.zeros((8, MIX), F32)
     dstate, later = scan_step(0, 1, first[1], dstate, later)
     upper[0] = upper[0]()
-    (part_1,) = run(input_back, False, first[1]["dconv"], first[1]["dgate"], wc0, wg0)
     lower_gate(0)
     gate0 = carrier.trade_grads(run(carrier.grad_gate, 0, *of(first, "normed", "dgate", "gated", "u")))
-    grads1 = run(natural_rows, upper, 16)
+    (part_1,) = run(input_back, False, first[1]["dconv"], first[1]["dgate"], wc0, wg0)
     gate0 = carrier.send(gate0)
     dstate, later = scan_step(0, 0, first[0], dstate, later)
     conv0 = carrier.trade_grads(run(carrier.grad_conv, 0, *of(first, "normed", "dconv")))
     (part_0,) = run(input_back, False, first[0]["dconv"], first[0]["dgate"], wc0, wg0)
     conv0 = carrier.send(conv0)
     part = scatter_start(*run(collect, [far(part_0), far(part_1)]))
+    grads1 = run(natural_rows, upper, 16)
     part = scatter_slots(run, *part)
     carrier.early(conv1, gate1, gate0)
     branch = jnp.zeros((piece, d), F32)

time: 558 us -> 554 us (level)
    unnamed x462 -> x478, local copies, waits for them, and re-layouts: 46.5 us -> 45.8 us
  transfers between devices with their start and end apart: 92 -> 92, of which waited for: 39 -> 37; matrix products, arithmetic and copies ran while one was open for 5% -> 4% of each run, Pallas kernels for 39% -> 39%
where the time goes in v1:
time: 554 us; the launch traced here: 549 us
  Pallas kernels  249 us (45%)
  waiting for transfers between devices  140 us (25%)
  starting transfers between devices  79.4 us (14%)
  local copies, waits for them, and re-layouts  53.3 us (10%)
  between operations  17.3 us (3%)
  other arithmetic  10.2 us (2%)
    pallas_call x63, Pallas kernels, call(): pl.pallas_call(kernel, grid_spec=pltpu.PrefetchScalarGridSpec(num_scalar_...  249 us
    ppermute x66, waiting for transfers between devices, flip(): return lax.ppermute(x, 'ctx', [(i, i ^ bits) for i in range(CTX)])  113 us
    ppermute x66, starting transfers between devices, flip(): return lax.ppermute(x, 'ctx', [(i, i ^ bits) for i in range(CTX)])  73.9 us
    unnamed x478, local copies, waits for them, and re-layouts  45.8 us
    all_gather x4, waiting for transfers between devices, gathered(): return lax.all_gather(x, 'dp', axis=0)  17.3 us
  transfers between devices with their start and end apart: 92, of which 37 were waited for; matrix products, arithmetic and copies ran while one was open for 4% of the time, Pallas kernels for 39%

profile of v1, /device:TPU:0, one launch (start us, length us, event | category | flops | bytes accessed | tf_op | source)
XLA Modules:
  0.0 549.4 jit_solution(243756319921315473)
XLA Ops:
  16.3 5.3 collective-permute-done.refs_1_
  21.6 5.9 %collective-permute-done.1.refs_2_ = bf16[96,1280]{1,0:T(8,128)(2,1)S(1)} collective-permute-done((bf16[96,1280]{1,0:T(8,128)(2,1)S(1)}, bf16[96,1280]{1,0:T(8,128)(2,1)S(1)}, u32[]{:S(2)}, u32[]{:S(2)}) %collective-permute-start.1) | collective-permute-done | bytes 245792 | tf_op jit(solution)/shard_map/ppermute | solution.py:48
  39.0 16.9 %collective-permute-done.5.refs_3_ = bf16[96,768]{1,0:T(8,128)(2,1)S(1)} collective-permute-done((bf16[96,768]{1,0:T(8,128)(2,1)}, bf16[96,768]{1,0:T(8,128)(2,1)S(1)}, u32[]{:S(2)}, u32[]{:S(2)}) %collective-permute-start.5) | collective-permute-done | bytes 147488 | tf_op jit(solution)/shard_map/ppermute | solution.py:48
  64.1 7.2 %collective-permute-done.8 = bf16[128,1536]{1,0:T(8,128)(2,1)S(1)} collective-permute-done((bf16[128,1536]{1,0:T(8,128)(2,1)S(1)}, bf16[128,1536]{1,0:T(8,128)(2,1)S(1)}, u32[]{:S(2)}, u32[]{:S(2)}) %collective-permute-start.8) | collective-permute-done | bytes 393248 | tf_op jit(solution)/shard_map/ppermute | solution.py:48
  85.5 5.1 project.4
  90.7 7.6 %scan_rows.4 = (f32[512,768]{1,0:T(8,128)S(1)}, f32[512,768]{1,0:T(8,128)}, f32[128,768]{1,0:T(8,128)S(1)}, bf16[16,1024]{1,0:T(8,128)(2,1)S(1)}) custom-call(s32[7]{0:T(128)S(1)} %pad_add_fusion.sp, bf16[512,1024]{1,0:T(8,128)(2,1)S(1)} %get-tuple-element.310.ci_ref.prev_ref, f32[512,128]{1,0:T(8,128)S(1)} %get-tuple-element.311.raw_ref, ...), custom_call_target="tpu_custom_call" | custom-call | flops 8000000000 | bytes 1 | tf_op jit(solution)/shard_map/scan_rows/pallas_call | solution.py:114
  99.6 4.4 project.5
  104.0 7.8 %scan_rows.5 = (f32[512,768]{1,0:T(8,128)S(1)}, f32[512,768]{1,0:T(8,128)}, f32[128,768]{1,0:T(8,128)}, bf16[16,1024]{1,0:T(8,128)(2,1)}) custom-call(s32[7]{0:T(128)S(1)} %pad_add_fusion.sp, bf16[512,1024]{1,0:T(8,128)(2,1)S(1)} %get-tuple-element.316.ci_ref.prev_ref, f32[512,128]{1,0:T(8,128)S(1)} %get-tuple-element.317.raw_ref, ...), custom_call_target="tpu_custom_call" | custom-call | flops 8000000000 | bytes 1 | tf_op jit(solution)/shard_map/scan_rows/pallas_call | solution.py:114
  113.9 12.8 %all-gather.11.cloned.1.call-done = bf16[16,96,768]{2,1,0:T(8,128)(2,1)} async-done(((bf16[4,96,768]{2,1,0:T(8,128)(2,1)}), bf16[16,96,768]{2,1,0:T(8,128)(2,1)}) %all-gather.11.cloned.1.call-update) | async-done | bytes 2359312 | tf_op jit(solution)/shard_map/all_gather | solution.py:1221
  146.8 4.5 out_rows.5
  159.4 6.9 %collective-permute-done.20.refs_8_ = bf16[64,1536]{1,0:T(8,128)(2,1)S(1)} collective-permute-done((bf16[64,1536]{1,0:T(8,128)(2,1)S(1)}, bf16[64,1536]{1,0:T(8,128)(2,1)S(1)}, u32[]{:S(2)}, u32[]{:S(2)}) %collective-permute-start.20) | collective-permute-done | bytes 196640 | tf_op jit(solution)/shard_map/ppermute | solution.py:48
  202.6 4.4 collective-permute-done.32.refs_1_.refs_6_
  210.4 7.7 %scan_rows.6 = (f32[512,768]{1,0:T(8,128)S(1)}, f32[512,768]{1,0:T(8,128)}, f32[128,768]{1,0:T(8,128)S(1)}, bf16[16,1024]{1,0:T(8,128)(2,1)S(1)}) custom-call(s32[7]{0:T(128)S(1)} %pad_add_fusion.sp, bf16[512,1024]{1,0:T(8,128)(2,1)S(1)} %get-tuple-element.374.ci_ref.prev_ref, f32[512,128]{1,0:T(8,128)S(1)} %get-tuple-element.375.raw_ref, ...), custom_call_target="tpu_custom_call" | custom-call | flops 8000000000 | bytes 1 | tf_op jit(solution)/shard_map/scan_rows/pallas_call | solution.py:114
  226.6 7.8 %scan_rows.7 = (f32[512,768]{1,0:T(8,128)S(1)}, f32[512,768]{1,0:T(8,128)}, f32[128,768]{1,0:T(8,128)}, bf16[16,1024]{1,0:T(8,128)(2,1)}) custom-call(s32[7]{0:T(128)S(1)} %pad_add_fusion.sp, bf16[512,1024]{1,0:T(8,128)(2,1)S(1)} %get-tuple-element.383.ci_ref.prev_ref, f32[512,128]{1,0:T(8,128)S(1)} %get-tuple-element.384.raw_ref, ...), custom_call_target="tpu_custom_call" | custom-call | flops 8000000000 | bytes 1 | tf_op jit(solution)/shard_map/scan_rows/pallas_call | solution.py:114
  236.3 5.7 %out_rows.6 = (f32[512,768]{1,0:T(8,128)S(1)}, f32[8,512]{1,0:T(8,128)S(1)}, bf16[512,1536]{1,0:T(8,128)(2,1)S(1)}) custom-call(s32[7]{0:T(128)S(1)} %pad_add_fusion.sp, bf16[4,2,128,1536]{3,2,1,0:T(8,128)(2,1)} %bitcast.13.refs_0_.refs_1_.refs_2_.refs_3_.refs_4_.refs_6_, bf16[4,2,128,1536]{3,2,1,0:T(8,128)(2,1)} %bitcast.13.refs_0_.refs_1_.refs_2_.refs_3_.refs_4_.refs_6_, ...), custom_call_target="tpu_custom_call" | custom-call | flops 4000000000 | bytes 1 | tf_op jit(solution)/shard_map/out_rows/pallas_call | solution.py:114
  242.0 5.7 %out_rows.7 = (f32[512,768]{1,0:T(8,128)S(1)}, f32[16,512]{1,0:T(8,128)S(1)}, bf16[512,1536]{1,0:T(8,128)(2,1)S(1)}) custom-call(s32[7]{0:T(128)S(1)} %pad_add_fusion.sp, f32[8,512]{1,0:T(8,128)S(1)} %get-tuple-element.396.refs_0_, bf16[4,2,128,1536]{3,2,1,0:T(8,128)(2,1)} %bitcast.13.refs_0_.refs_1_.refs_2_.refs_3_.refs_4_.refs_6_, ...), custom_call_target="tpu_custom_call" | custom-call | flops 4000000000 | bytes 1 | tf_op jit(solution)/shard_map/out_rows/pallas_call | solution.py:114
  259.7 4.1 gate_back.5
  263.9 8.5 %grad_gate.2 = (bf16[4,4,96,768]{3,2,1,0:T(8,128)(2,1)S(1)}, bf16[4,4,96,768]{3,2,1,0:T(8,128)(2,1)S(1)}) custom-call(s32[7]{0:T(128)S(1)} %pad_add_fusion.sp, bf16[512,1536]{1,0:T(8,128)(2,1)S(1)} %copy-done.34, bf16[512,1536]{1,0:T(8,128)(2,1)S(1)} %get-tuple-element.381.refs_5_.refs_1_.n1_ref, bf16[512,768]{1,0:T(8,128)(2,1)S(1)} %get-tuple-element.409.refs_2_.dg_ref, ...), custom_call_target="tpu_custom_call" | custom-call | flops 8000000000 | bytes 1 | tf_op jit(solution)/shard_map/grad_gate/pallas_call | solution.py:114
  273.7 15.7 %scan_back.4 = (bf16[512,1152]{1,0:T(8,128)(2,1)S(1)}, f32[8,1024]{1,0:T(8,128)S(1)}, f32[8,128]{1,0:T(8,128)S(1)}, f32[128,768]{1,0:T(8,128)S(1)}, f32[8,1024]{1,0:T(8,128)S(1)}) custom-call(s32[7]{0:T(128)S(1)} %pad_add_fusion.sp, bf16[512,1024]{1,0:T(8,128)(2,1)S(1)} %get-tuple-element.383.ci_ref.prev_ref, ...), custom_call_target="tpu_custom_call" | custom-call | flops 16000000000 | bytes 1 | tf_op jit(solution)/shard_map/scan_back/pallas_call | solution.py:114
  309.6 16.6 %scan_back.5 = (bf16[512,1152]{1,0:T(8,128)(2,1)S(1)}, f32[8,1024]{1,0:T(8,128)S(1)}, f32[8,128]{1,0:T(8,128)S(1)}, f32[128,768]{1,0:T(8,128)}, f32[8,1024]{1,0:T(8,128)}) custom-call(s32[7]{0:T(128)S(1)} %pad_add_fusion.sp, bf16[512,1024]{1,0:T(8,128)(2,1)S(1)} %copy-done.197, bf16[512,1024]{1,0:T(8,128)(2,1)S(1)} %copy-done.197, ...), custom_call_target="tpu_custom_call" | custom-call | flops 16000000000 | bytes 1 | tf_op jit(solution)/shard_map/scan_back/pallas_call | solution.py:114
  344.9 5.9 %grad_conv.2 = (bf16[4,4,96,640]{3,2,1,0:T(8,128)(2,1)S(1)}, bf16[4,4,96,640]{3,2,1,0:T(8,128)(2,1)S(1)}) custom-call(s32[7]{0:T(128)S(1)} %pad_add_fusion.sp, bf16[512,1536]{1,0:T(8,128)(2,1)S(1)} %copy-done.35, bf16[512,1536]{1,0:T(8,128)(2,1)S(1)} %copy-done.37, bf16[512,1152]{1,0:T(8,128)(2,1)S(1)} %get-tuple-element.433.dc_ref.d0_ref, ...), custom_call_target="tpu_custom_call" | custom-call | flops 6000000000 | bytes 1 | tf_op jit(solution)/shard_map/grad_conv/pallas_call | solution.py:114
  350.8 4.8 collective-permute-done.50.refs_1_.refs_10_.refs_6_
  361.6 4.4 collective-permute-done.55.refs_4_.refs_9_
  382.0 17.5 %scan_back.6 = (bf16[512,1152]{1,0:T(8,128)(2,1)S(1)}, f32[8,1024]{1,0:T(8,128)S(1)}, f32[8,128]{1,0:T(8,128)S(1)}, f32[128,768]{1,0:T(8,128)S(1)}, f32[8,1024]{1,0:T(8,128)S(1)}) custom-call(s32[7]{0:T(128)S(1)} %pad_add_fusion.sp, bf16[512,1024]{1,0:T(8,128)(2,1)} %copy-done.140, bf16[512,1024]{1,0:T(8,128)(2,1)} %copy-done.140, f32[512,128]{1,0:T(8,128)} %copy-done.152, ...), custom_call_target="tpu_custom_call" | custom-call | flops 16000000000 | bytes 1 | tf_op jit(solution)/shard_map/scan_back/pallas_call | solution.py:114
  403.1 4.9 collective-permute-done.62.refs_4_
  411.0 8.1 %grad_gate.3 = (bf16[4,4,96,768]{3,2,1,0:T(8,128)(2,1)S(1)}, bf16[4,4,96,768]{3,2,1,0:T(8,128)(2,1)S(1)}) custom-call(s32[7]{0:T(128)S(1)} %pad_add_fusion.sp, bf16[512,1536]{1,0:T(8,128)(2,1)S(1)} %copy-done.132, bf16[512,1536]{1,0:T(8,128)(2,1)S(1)} %copy-done.136, bf16[512,768]{1,0:T(8,128)(2,1)S(1)} %get-tuple-element.479.refs_2_.dg_ref, ...), custom_call_target="tpu_custom_call" | custom-call | flops 8000000000 | bytes 1 | tf_op jit(solution)/shard_map/grad_gate/pallas_call | solution.py:114
  427.1 18.6 %scan_back.7 = (bf16[512,1152]{1,0:T(8,128)(2,1)S(1)}, f32[8,1024]{1,0:T(8,128)S(1)}, f32[8,128]{1,0:T(8,128)S(1)}, f32[128,768]{1,0:T(8,128)}, f32[8,1024]{1,0:T(8,128)}) custom-call(s32[7]{0:T(128)S(1)} %pad_add_fusion.sp, bf16[512,1024]{1,0:T(8,128)(2,1)} %copy-done.139, bf16[512,1024]{1,0:T(8,128)(2,1)} %copy-done.139, f32[512,128]{1,0:T(8,128)} %copy-done.151, ...), custom_call_target="tpu_custom_call" | custom-call | flops 16000000000 | bytes 1 | tf_op jit(solution)/shard_map/scan_back/pallas_call | solution.py:114
  445.8 5.9 %grad_conv.3 = (bf16[4,4,96,640]{3,2,1,0:T(8,128)(2,1)S(1)}, bf16[4,4,96,640]{3,2,1,0:T(8,128)(2,1)S(1)}) custom-call(s32[7]{0:T(128)S(1)} %pad_add_fusion.sp, bf16[512,1536]{1,0:T(8,128)(2,1)S(1)} %copy-done.133, bf16[512,1536]{1,0:T(8,128)(2,1)S(1)} %copy-done.137, bf16[512,1152]{1,0:T(8,128)(2,1)S(1)} %get-tuple-element.493.d0_ref.dc_ref, ...), custom_call_target="tpu_custom_call" | custom-call | flops 6000000000 | bytes 1 | tf_op jit(solution)/shard_map/grad_conv/pallas_call | solution.py:114
  466.8 16.7 %collective-permute-done.65.from_x_ref.refs_1_ = bf16[256,1536]{1,0:T(8,128)(2,1)S(1)} collective-permute-done((bf16[256,1536]{1,0:T(8,128)(2,1)S(1)}, bf16[256,1536]{1,0:T(8,128)(2,1)S(1)}, u32[]{:S(2)}, u32[]{:S(2)}) %collective-permute-start.65) | collective-permute-done | bytes 786464 | tf_op jit(solution)/shard_map/ppermute | solution.py:48
  494.1 4.6 collective-permute-done.67.refs_3_
  504.5 4.3 collective-permute-done.71.refs_2_
  513.1 4.2 collective-permute-done.79
  (737 shorter events, 271.6 us)
Async XLA Ops:
  7.2 68.0 %all-gather.9.cloned.1.call-start = ((), (), s32[]{:S(2)}) async-start(), calls=%async_computation.8 | async-start | bytes 2457600 | tf_op jit(solution)/shard_map/all_gather | solution.py:1221
  31.1 95.5 %all-gather.11.cloned.1.call-start = ((), (), s32[]{:S(2)}) async-start(), calls=%async_computation.9 | async-start | bytes 2949120 | tf_op jit(solution)/shard_map/all_gather | solution.py:1221
  31.3 28.4 %collective-permute-start.6 = (bf16[256,1536]{1,0:T(8,128)(2,1)S(1)}, bf16[256,1536]{1,0:T(8,128)(2,1)S(1)}, u32[]{:S(2)}, u32[]{:S(2)}) collective-permute-start(bf16[256,1536]{1,0:T(8,128)(2,1)S(1)} %dynamic-slice_bitcast_fusion.1.refs_5_), channel_id=1, source_target_pairs={{0,1},{1,0},{2,3},{3,2},{4,5},{5,4},{6,7},{7,6},{8,9},{9,8},{10,11... | collective-permute-start | bytes 2359304 | tf_op jit(solution)/shard_map/ppermute | solution.py:48
  32.6 27.1 %collective-permute-start.7 = (bf16[256,1536]{1,0:T(8,128)(2,1)S(1)}, bf16[256,1536]{1,0:T(8,128)(2,1)S(1)}, u32[]{:S(2)}, u32[]{:S(2)}) collective-permute-start(bf16[256,1536]{1,0:T(8,128)(2,1)S(1)} %dynamic-slice_bitcast_fusion.1.refs_5_), channel_id=1, source_target_pairs={{0,2},{1,3},{2,0},{3,1},{4,6},{5,7},{6,4},{7,5},{8,10},{9,11},{10,... | collective-permute-start | bytes 2359304 | tf_op jit(solution)/shard_map/ppermute | solution.py:48
  33.4 22.5 %collective-permute-start.5 = (bf16[96,768]{1,0:T(8,128)(2,1)}, bf16[96,768]{1,0:T(8,128)(2,1)S(1)}, u32[]{:S(2)}, u32[]{:S(2)}) collective-permute-start(bf16[96,768]{1,0:T(8,128)(2,1)} %get-tuple-element.297), channel_id=1, source_target_pairs={{0,3},{1,2},{2,1},{3,0},{4,7},{5,6},{6,5},{7,4},{8,11},{9,10},{10,... | collective-permute-start | bytes 442376 | tf_op jit(solution)/shard_map/ppermute | solution.py:48
  34.8 23.4 %collective-permute-start.4 = (bf16[96,768]{1,0:T(8,128)(2,1)}, bf16[96,768]{1,0:T(8,128)(2,1)S(1)}, u32[]{:S(2)}, u32[]{:S(2)}) collective-permute-start(bf16[96,768]{1,0:T(8,128)(2,1)} %get-tuple-element.295), channel_id=1, source_target_pairs={{0,2},{1,3},{2,0},{3,1},{4,6},{5,7},{6,4},{7,5},{8,10},{9,11},{10,... | collective-permute-start | bytes 442376 | tf_op jit(solution)/shard_map/ppermute | solution.py:48
  36.4 21.8 %collective-permute-start.3 = (bf16[96,768]{1,0:T(8,128)(2,1)S(1)}, bf16[96,768]{1,0:T(8,128)(2,1)S(1)}, u32[]{:S(2)}, u32[]{:S(2)}) collective-permute-start(bf16[96,768]{1,0:T(8,128)(2,1)S(1)} %get-tuple-element.293), channel_id=1, source_target_pairs={{0,1},{1,0},{2,3},{3,2},{4,5},{5,4},{6,7},{7,6},{8,9},{9,8},{10,11... | collective-permute-start | bytes 442376 | tf_op jit(solution)/shard_map/ppermute | solution.py:48
  76.3 108.6 %all-gather.13.cloned.1.call-start = ((), (), s32[]{:S(2)}) async-start(), calls=%async_computation.10 | async-start | bytes 2457600 | tf_op jit(solution)/shard_map/all_gather | solution.py:1221
  79.3 33.7 %collective-permute-start.13 = (bf16[256,1536]{1,0:T(8,128)(2,1)S(1)}, bf16[256,1536]{1,0:T(8,128)(2,1)S(1)}, u32[]{:S(2)}, u32[]{:S(2)}) collective-permute-start(bf16[256,1536]{1,0:T(8,128)(2,1)S(1)} %dynamic-slice_bitcast_fusion), channel_id=1, source_target_pairs={{0,1},{1,0},{2,3},{3,2},{4,5},{5,4},{6,7},{7,6},{8,9},{9,8},{10,11... | collective-permute-start | bytes 2359304 | tf_op jit(solution)/shard_map/ppermute | solution.py:48
  80.9 33.0 %collective-permute-start.14 = (bf16[256,1536]{1,0:T(8,128)(2,1)S(1)}, bf16[256,1536]{1,0:T(8,128)(2,1)}, u32[]{:S(2)}, u32[]{:S(2)}) collective-permute-start(bf16[256,1536]{1,0:T(8,128)(2,1)S(1)} %dynamic-slice_bitcast_fusion), channel_id=1, source_target_pairs={{0,2},{1,3},{2,0},{3,1},{4,6},{5,7},{6,4},{7,5},{8,10},{9,11},{10,... | collective-permute-start | bytes 2359304 | tf_op jit(solution)/shard_map/ppermute | solution.py:48
  126.7 94.7 %all-gather.15.cloned.1.call-start = ((), (), s32[]{:S(2)}) async-start(), calls=%async_computation.11 | async-start | bytes 2949120 | tf_op jit(solution)/shard_map/all_gather | solution.py:1221
  145.6 25.8 %collective-permute-start.25 = (bf16[128,1536]{1,0:T(8,128)(2,1)}, bf16[128,1536]{1,0:T(8,128)(2,1)}, u32[]{:S(2)}, u32[]{:S(2)}) collective-permute-start(bf16[128,1536]{1,0:T(8,128)(2,1)} %slice.50), channel_id=1, source_target_pairs={{0,1},{1,0},{2,3},{3,2},{4,5},{5,4},{6,7},{7,6},{8,9},{9,8},{10,11... | collective-permute-start | bytes 1179656 | tf_op jit(solution)/shard_map/ppermute | solution.py:48
  146.1 28.5 %collective-permute-start.26 = (bf16[128,1536]{1,0:T(8,128)(2,1)}, bf16[128,1536]{1,0:T(8,128)(2,1)}, u32[]{:S(2)}, u32[]{:S(2)}) collective-permute-start(bf16[128,1536]{1,0:T(8,128)(2,1)} %slice.51), channel_id=1, source_target_pairs={{0,2},{1,3},{2,0},{3,1},{4,6},{5,7},{6,4},{7,5},{8,10},{9,11},{10,... | collective-permute-start | bytes 1179656 | tf_op jit(solution)/shard_map/ppermute | solution.py:48
  158.5 329.8 %reduce-scatter.7.cloned.1.call-start = ((), (), s32[]{:S(2)}) async-start(), calls=%async_computation.5 | async-start | bytes 2949120 | tf_op jit(solution)/shard_map/reduce_scatter | solution.py:1254
  158.7 17.7 %collective-permute-start.22 = (bf16[144,1536]{1,0:T(8,128)(2,1)}, bf16[144,1536]{1,0:T(8,128)(2,1)S(1)}, u32[]{:S(2)}, u32[]{:S(2)}) collective-permute-start(bf16[144,1536]{1,0:T(8,128)(2,1)} %get-tuple-element.349), channel_id=1, source_target_pairs={{0,2},{1,3},{2,0},{3,1},{4,6},{5,7},{6,4},{7,5},{8,10},{9,11},{10,... | collective-permute-start | bytes 1327112 | tf_op jit(solution)/shard_map/ppermute | solution.py:48
  272.4 23.9 %collective-permute-start.42 = (bf16[4,4,96,768]{3,2,1,0:T(8,128)(2,1)S(1)}, bf16[4,4,96,768]{3,2,1,0:T(8,128)(2,1)S(1)}, u32[]{:S(2)}, u32[]{:S(2)}) collective-permute-start(bf16[4,4,96,768]{3,2,1,0:T(8,128)(2,1)S(1)} %get-tuple-element.426), channel_id=1, source_target_pairs={{0,16},{16,0},{1,17},{17,1},{2,18},{18,2},{3,19},{19,3},{4,20},{20... | collective-permute-start | bytes 7077896 | tf_op jit(solution)/shard_map/ppermute | solution.py:44
  272.5 20.0 %collective-permute-start.40 = (bf16[256,1536]{1,0:T(8,128)(2,1)S(1)}, bf16[256,1536]{1,0:T(8,128)(2,1)S(1)}, u32[]{:S(2)}, u32[]{:S(2)}) collective-permute-start(bf16[256,1536]{1,0:T(8,128)(2,1)S(1)} %get-tuple-element.420), channel_id=1, source_target_pairs={{0,1},{1,0},{2,3},{3,2},{4,5},{5,4},{6,7},{7,6},{8,9},{9,8},{10,11... | collective-permute-start | bytes 2359304 | tf_op jit(solution)/shard_map/ppermute | solution.py:48
  273.1 19.6 %collective-permute-start.41 = (bf16[256,1536]{1,0:T(8,128)(2,1)S(1)}, bf16[256,1536]{1,0:T(8,128)(2,1)S(1)}, u32[]{:S(2)}, u32[]{:S(2)}) collective-permute-start(bf16[256,1536]{1,0:T(8,128)(2,1)S(1)} %get-tuple-element.421), channel_id=1, source_target_pairs={{0,2},{1,3},{2,0},{3,1},{4,6},{5,7},{6,4},{7,5},{8,10},{9,11},{10,... | collective-permute-start | bytes 2359304 | tf_op jit(solution)/shard_map/ppermute | solution.py:48
  294.3 31.9 %collective-permute-start.43 = (bf16[128,1536]{1,0:T(8,128)(2,1)}, bf16[128,1536]{1,0:T(8,128)(2,1)}, u32[]{:S(2)}, u32[]{:S(2)}) collective-permute-start(bf16[128,1536]{1,0:T(8,128)(2,1)} %get-tuple-element.424), channel_id=1, source_target_pairs={{0,1},{1,0},{2,3},{3,2},{4,5},{5,4},{6,7},{7,6},{8,9},{9,8},{10,11... | collective-permute-start | bytes 1179656 | tf_op jit(solution)/shard_map/ppermute | solution.py:48
  295.7 30.5 %collective-permute-start.44 = (bf16[128,1536]{1,0:T(8,128)(2,1)}, bf16[128,1536]{1,0:T(8,128)(2,1)}, u32[]{:S(2)}, u32[]{:S(2)}) collective-permute-start(bf16[128,1536]{1,0:T(8,128)(2,1)} %get-tuple-element.435), channel_id=1, source_target_pairs={{0,2},{1,3},{2,0},{3,1},{4,6},{5,7},{6,4},{7,5},{8,10},{9,11},{10,... | collective-permute-start | bytes 1179656 | tf_op jit(solution)/shard_map/ppermute | solution.py:48
  299.0 189.4 %reduce-scatter.5.cloned.1.call-start = ((), (), s32[]{:S(2)}) async-start(), calls=%async_computation.4 | async-start | bytes 2457600 | tf_op jit(solution)/shard_map/reduce_scatter | solution.py:1254
  307.7 22.9 %collective-permute-start.46 = (bf16[128,1536]{1,0:T(8,128)(2,1)S(1)}, bf16[128,1536]{1,0:T(8,128)(2,1)S(1)}, u32[]{:S(2)}, u32[]{:S(2)}) collective-permute-start(bf16[128,1536]{1,0:T(8,128)(2,1)S(1)} %get-tuple-element.438), channel_id=1, source_target_pairs={{0,1},{1,0},{2,3},{3,2},{4,5},{5,4},{6,7},{7,6},{8,9},{9,8},{10,11... | collective-permute-start | bytes 1179656 | tf_op jit(solution)/shard_map/ppermute | solution.py:48
  308.1 22.6 %collective-permute-start.47 = (bf16[128,1536]{1,0:T(8,128)(2,1)S(1)}, bf16[128,1536]{1,0:T(8,128)(2,1)S(1)}, u32[]{:S(2)}, u32[]{:S(2)}) collective-permute-start(bf16[128,1536]{1,0:T(8,128)(2,1)S(1)} %get-tuple-element.439), channel_id=1, source_target_pairs={{0,2},{1,3},{2,0},{3,1},{4,6},{5,7},{6,4},{7,5},{8,10},{9,11},{10,... | collective-permute-start | bytes 1179656 | tf_op jit(solution)/shard_map/ppermute | solution.py:48
  337.6 19.0 %collective-permute-start.52 = (bf16[128,1536]{1,0:T(8,128)(2,1)S(1)}, bf16[128,1536]{1,0:T(8,128)(2,1)S(1)}, u32[]{:S(2)}, u32[]{:S(2)}) collective-permute-start(bf16[128,1536]{1,0:T(8,128)(2,1)S(1)} %get-tuple-element.453), channel_id=1, source_target_pairs={{0,1},{1,0},{2,3},{3,2},{4,5},{5,4},{6,7},{7,6},{8,9},{9,8},{10,11... | collective-permute-start | bytes 1179656 | tf_op jit(solution)/shard_map/ppermute | solution.py:48
  338.2 18.4 %collective-permute-start.53 = (bf16[128,1536]{1,0:T(8,128)(2,1)S(1)}, bf16[128,1536]{1,0:T(8,128)(2,1)S(1)}, u32[]{:S(2)}, u32[]{:S(2)}) collective-permute-start(bf16[128,1536]{1,0:T(8,128)(2,1)S(1)} %get-tuple-element.454), channel_id=1, source_target_pairs={{0,2},{1,3},{2,0},{3,1},{4,6},{5,7},{6,4},{7,5},{8,10},{9,11},{10,... | collective-permute-start | bytes 1179656 | tf_op jit(solution)/shard_map/ppermute | solution.py:48
  379.7 21.3 %collective-permute-start.59 = (bf16[144,1536]{1,0:T(8,128)(2,1)S(1)}, bf16[144,1536]{1,0:T(8,128)(2,1)S(1)}, u32[]{:S(2)}, u32[]{:S(2)}) collective-permute-start(bf16[144,1536]{1,0:T(8,128)(2,1)S(1)} %get-tuple-element.469.refs_0_.refs_9_), channel_id=1, source_target_pairs={{0,1},{1,0},{2,3},{3,2},{4,5},{5,4},{6,7},{7,6},{8,9},{9,8},{10,11... | collective-permute-start | bytes 1327112 | tf_op jit(solution)/shard_map/ppermute | solution.py:48
  380.8 20.2 %collective-permute-start.60 = (bf16[144,1536]{1,0:T(8,128)(2,1)S(1)}, bf16[144,1536]{1,0:T(8,128)(2,1)S(1)}, u32[]{:S(2)}, u32[]{:S(2)}) collective-permute-start(bf16[144,1536]{1,0:T(8,128)(2,1)S(1)} %get-tuple-element.469.refs_0_.refs_9_), channel_id=1, source_target_pairs={{0,2},{1,3},{2,0},{3,1},{4,6},{5,7},{6,4},{7,5},{8,10},{9,11},{10,... | collective-permute-start | bytes 1327112 | tf_op jit(solution)/shard_map/ppermute | solution.py:48
  381.9 106.5 %reduce-scatter.9.cloned.1.call-start = ((), (), s32[]{:S(2)}) async-start(), calls=%async_computation.6 | async-start | bytes 2949120 | tf_op jit(solution)/shard_map/reduce_scatter | solution.py:1254
  427.0 92.1 %reduce-scatter.11.cloned.1.call-start = ((), (), s32[]{:S(2)}) async-start(), calls=%async_computation.7 | async-start | bytes 2457600 | tf_op jit(solution)/shard_map/reduce_scatter | solution.py:1254
  464.0 19.5 %collective-permute-start.65 = (bf16[256,1536]{1,0:T(8,128)(2,1)S(1)}, bf16[256,1536]{1,0:T(8,128)(2,1)S(1)}, u32[]{:S(2)}, u32[]{:S(2)}) collective-permute-start(bf16[256,1536]{1,0:T(8,128)(2,1)S(1)} %get-tuple-element.503), channel_id=1, source_target_pairs={{0,1},{1,0},{2,3},{3,2},{4,5},{5,4},{6,7},{7,6},{8,9},{9,8},{10,11... | collective-permute-start | bytes 2359304 | tf_op jit(solution)/shard_map/ppermute | solution.py:48
  464.9 19.2 %collective-permute-start.66 = (bf16[256,1536]{1,0:T(8,128)(2,1)S(1)}, bf16[256,1536]{1,0:T(8,128)(2,1)S(1)}, u32[]{:S(2)}, u32[]{:S(2)}) collective-permute-start(bf16[256,1536]{1,0:T(8,128)(2,1)S(1)} %get-tuple-element.504), channel_id=1, source_target_pairs={{0,2},{1,3},{2,0},{3,1},{4,6},{5,7},{6,4},{7,5},{8,10},{9,11},{10,... | collective-permute-start | bytes 2359304 | tf_op jit(solution)/shard_map/ppermute | solution.py:48
  511.2 19.4 %collective-permute-start.69 = (bf16[256,1536]{1,0:T(8,128)(2,1)}, bf16[256,1536]{1,0:T(8,128)(2,1)}, u32[]{:S(2)}, u32[]{:S(2)}) collective-permute-start(bf16[256,1536]{1,0:T(8,128)(2,1)} %broadcast_select_fusion), channel_id=1, source_target_pairs={{0,16},{16,0},{1,17},{17,1},{2,18},{18,2},{3,19},{19,3},{4,20},{20... | collective-permute-start | bytes 2359304 | tf_op jit(solution)/shard_map/ppermute | solution.py:44
  (295 other events, 2886.2 us)
Sparse Core Ops, SparseCore 0:
  31.3 43.8 all-gather.8
  77.3 49.3 all-gather.10
  128.3 42.3 all-gather.12
  172.1 49.3 all-gather.14
  299.1 45.9 reduce-scatter.6
  382.0 39.2 reduce-scatter.4
  427.2 45.9 reduce-scatter.8
  475.4 40.9 reduce-scatter.10
